TPU v7x, 512 devices: a whole 4x8x8 slice. The times are simulated.
512 devices in a mesh: row: 32 (over y, x_lo, core), col: 16 (over z, x_hi).
Axes of the slice: x: 4 (x_hi: 2, x_lo: 2; x = x_hi * 2 + x_lo), y: 8, z: 8, core: 2. Of those that a mesh axis runs over, the one named last changes fastest.
Arguments:
- states: bfloat16 [32768, 512], P(('row', 'col')), may hold values from -1 to 1
- targets: float32 [32, 32768], P(None, ('row', 'col')), may hold values from -6 to 6
- start_coef: float32 [32, 32768], P(None, ('row', 'col')), may hold values from -4 to 4
- washout: int32 [32768], P(('row', 'col')), may hold values 0 or 1
Outputs:
- coef: float32 [32, 32768], P(None, ('row', 'col'))
- residual: float32 [32, 32768], P(None, ('row', 'col'))
All inputs are finite; a program needn't handle non-finite values. No bound on the sum of `washout` on one device may be relied on, other than what follows from the above.
Results may differ from a plain program's by a relative error of at most 0.0003.
Values may be sent and summed in bfloat16 or wider, within the bound.
A program may use at most 64 MiB of HBM per device.

v0:
```python
import jax
import jax.numpy as jnp
from jax import lax
from jax.sharding import PartitionSpec as P

ridge_value = 1.0


def kernel_tile(row_states, row_norm, col_states):
    col_f = col_states.astype(jnp.float32)
    col_norm = jnp.sum(col_f * col_f, axis=1)
    cross = lax.dot_general(
        row_states, col_states, (((1,), (1,)), ((), ())), preferred_element_type=jnp.float32
    )
    return jnp.exp(-(row_norm[:, None] + col_norm[None, :] - 2.0 * cross) / row_states.shape[1])


def local(states, targets, start_coef, washout):
    mask = washout.astype(jnp.float32)
    row_states = lax.all_gather(states, "col", axis=0, tiled=True)
    row_f = row_states.astype(jnp.float32)
    row_norm = jnp.sum(row_f * row_f, axis=1)
    col_states = lax.all_gather(states, "row", axis=0, tiled=True)
    tile = kernel_tile(row_states, row_norm, col_states)

    def apply_operator(vector):
        masked = vector * mask[None, :]
        whole = lax.all_gather(masked, "row", axis=1, tiled=True)
        partial_sum = lax.dot_general(
            whole, tile, (((1,), (1,)), ((), ())), precision=lax.Precision.HIGHEST
        )
        owned = lax.psum_scatter(partial_sum, "col", scatter_dimension=1, tiled=True)
        return mask[None, :] * owned + ridge_value * vector

    start = mask[None, :] * targets - apply_operator(start_coef)
    local_squares = jnp.sum(start * start, axis=1)
    squares = lax.psum(local_squares, ("row", "col"))
    image = apply_operator(start)
    bending = lax.psum(jnp.sum(start * image, axis=1), ("row", "col"))
    alpha = squares / bending
    coef = start_coef + alpha[:, None] * start
    residual = start - alpha[:, None] * image
    return (coef, residual)


def solution(mesh):
    return jax.shard_map(
        local,
        mesh=mesh,
        in_specs=(
            P(("row", "col"), None),
            P(None, ("row", "col")),
            P(None, ("row", "col")),
            P(("row", "col")),
        ),
        out_specs=(P(None, ("row", "col")), P(None, ("row", "col"))),
        check_vma=False,
    )
```

profile of v0, /device:TPU:1, one launch (start us, length us, event | category | flops | bytes accessed | tf_op | source)
XLA Modules:
  0.0 743.3 jit_solution(7352962130659864154)
XLA Ops:
  7.2 0.0 all-gather.5.cloned.1.call-start
  7.2 0.7 all-gather.5.cloned.1.call-update
  7.9 0.0 all-gather.7.cloned.1.call-start
  7.9 0.7 all-gather.7.cloned.1.call-update
  8.6 0.0 reduce-scatter.7.cloned.1.call-start
  8.7 0.7 convert_element_type.9
  9.4 0.7 multiply_bitcast_fusion.1
  10.1 38.6 %all-gather = f32[32,64,32]{1,2,0:T(8,128)S(1)} all-gather(f32[1,64,32]{1,2,0:T(8,128)S(1)} %multiply_bitcast_fusion.1), channel_id=1, replica_groups=mesh['row'=32,'col'=16] {'row'}, dimensions={0}, use_global_device_ids=true | all-gather | bytes 270336 | tf_op jit(solution)/shard_map/all_gather | solution.py:28
  48.7 0.3 copy.8
  49.0 0.2 reshape.9
  49.2 48.7 %all-gather.5.cloned.1.call-done = bf16[1024,512]{1,0:T(8,128)(2,1)} async-done(((bf16[64,512]{1,0:T(8,128)(2,1)}), bf16[1024,512]{1,0:T(8,128)(2,1)}) %all-gather.5.cloned.1.call-update) | async-done | bytes 1048592 | tf_op jit(solution)/shard_map/all_gather | solution.py:20
  97.9 1.5 multiply_reduce_fusion.1
  99.4 68.1 %all-gather.7.cloned.1.call-done = bf16[2048,512]{1,0:T(8,128)(2,1)} async-done(((bf16[64,512]{1,0:T(8,128)(2,1)}), bf16[2048,512]{1,0:T(8,128)(2,1)}) %all-gather.7.cloned.1.call-update) | async-done | bytes 2097168 | tf_op jit(solution)/shard_map/all_gather | solution.py:23
  167.5 0.0 copy-start
  167.5 4.4 fusion.16
  172.0 0.0 copy-done
  172.0 0.0 copy-start.3
  172.0 0.0 copy-start.1
  172.0 0.0 copy-start.2
  172.0 0.5 multiply_reduce_fusion
  172.5 2.7 copy-done.3
  175.2 7.6 %fusion.10 = f32[1024,32]{1,0:T(8,128)} fusion(f32[2048,32]{0,1:T(8,128)S(1)} %reshape.9, f32[1024,2048]{1,0:T(8,128)S(1)} %fusion.16, f32[2048]{0:T(1024)S(1)} %multiply_reduce_fusion, f32[1024]{0:T(1024)S(1)} %multiply_reduce_fusion.1), kind=kOutput, calls=%fused_computation.13 | convolution fusion | flops 815792128 | bytes 8794112
  182.8 0.0 reduce-scatter.7.cloned.1.call-update
  182.9 0.0 reduce-scatter.9.cloned.1.call-start
  182.9 201.7 %reduce-scatter.7.cloned.1.call-done = f32[64,32]{1,0:T(8,128)} async-done(((f32[1024,32]{1,0:T(8,128)}), f32[64,32]{1,0:T(8,128)}) %reduce-scatter.7.cloned.1.call-update) | async-done | bytes 8208
  384.7 0.8 copy.11
  385.5 0.0 copy-done.1
  385.5 0.0 copy-done.2
  385.5 40.5 %all-gather.1 = f32[32,64,32]{1,2,0:T(8,128)S(1)} all-gather(f32[1,64,32]{1,2,0:T(8,128)S(1)} %get-tuple-element.6), channel_id=1, replica_groups=mesh['row'=32,'col'=16] {'row'}, dimensions={0}, use_global_device_ids=true | all-gather | bytes 270336 | tf_op jit(solution)/shard_map/all_gather | solution.py:28
  426.0 0.3 copy.9
  426.3 0.2 reshape.11
  426.5 10.0 %fusion.11 = f32[1024,32]{1,0:T(8,128)} fusion(f32[2048,32]{0,1:T(8,128)S(1)} %reshape.11, f32[1024,2048]{1,0:T(8,128)} %copy-done.3, f32[2048]{0:T(1024)S(1)} %multiply_reduce_fusion, f32[1024]{0:T(1024)S(1)} %multiply_reduce_fusion.1), kind=kOutput, calls=%fused_computation.14 | convolution fusion | flops 815792128 | bytes 8794112
  436.5 0.0 reduce-scatter.9.cloned.1.call-update
  436.6 198.3 %reduce-scatter.9.cloned.1.call-done = f32[64,32]{1,0:T(8,128)} async-done(((f32[1024,32]{1,0:T(8,128)}), f32[64,32]{1,0:T(8,128)}) %reduce-scatter.9.cloned.1.call-update) | async-done | bytes 8208
  634.9 0.8 copy.13
  635.7 0.1 multiply_reduce_fusion.2
  635.8 100.2 %all-reduce = (f32[32]{0:T(128)S(1)}, f32[32]{0:T(128)S(1)}) all-reduce(f32[32]{0:T(128)S(1)} %get-tuple-element.3, f32[32]{0:T(128)S(1)} %get-tuple-element.2), channel_id=1, replica_groups=mesh['row'=32,'col'=16] {'row','col'}, use_global_device_ids=true, to_apply=%region_4.0 | all-reduce | flops 64 | bytes 512 | tf_op jit(solution)/shard_map/psum | solution.py:37
  736.1 0.7 multiply_subtract_fusion
  (2 shorter events, 0.0 us)
Async XLA Ops:
  7.2 90.7 %all-gather.5.cloned.1.call-start = ((), (), s32[]{:S(2)}) async-start(), calls=%async_computation.2 | async-start | bytes 1114112 | tf_op jit(solution)/shard_map/all_gather | solution.py:20
  7.9 159.6 %all-gather.7.cloned.1.call-start = ((), (), s32[]{:S(2)}) async-start(), calls=%async_computation.3 | async-start | bytes 2162688 | tf_op jit(solution)/shard_map/all_gather | solution.py:23
  8.6 376.0 %reduce-scatter.7.cloned.1.call-start = ((), (), s32[]{:S(2)}) async-start(), calls=%async_computation.4 | async-start | bytes 557056
  167.5 4.4 copy-start
  172.0 3.2 copy-start.3
  172.0 213.5 %copy-start.1 = (f32[32,64]{1,0:T(8,128)S(1)}, f32[32,64]{1,0:T(8,128)}, u32[]{:S(2)}) copy-start(f32[32,64]{1,0:T(8,128)} %param.6) | copy-start | bytes 24580
  172.0 213.5 %copy-start.2 = (f32[32,64]{1,0:T(8,128)S(1)}, f32[32,64]{1,0:T(8,128)}, u32[]{:S(2)}) copy-start(f32[32,64]{1,0:T(8,128)} %param.5) | copy-start | bytes 24580
  182.9 452.0 %reduce-scatter.9.cloned.1.call-start = ((), (), s32[]{:S(2)}) async-start(), calls=%async_computation.5 | async-start | bytes 557056
Sparse Core Ops, SparseCore 0:
  11.2 86.6 all-gather.4
  100.0 67.4 all-gather.6
  183.0 201.6 reduce-scatter.6
  436.7 198.1 reduce-scatter.8
where the time goes:
time: 744 us; the launch traced here: 743 us
  waiting for transfers between devices  518 us (70%)
  blocking collectives  179 us (24%)
  matrix products  22.1 us (3%)
  between operations  13.8 us (2%)
    unnamed x6, waiting for transfers between devices  401 us
    psum x1, blocking collectives, local(): squares = lax.psum(local_squares, ('row', 'col'))  100 us
    all_gather x2, blocking collectives, apply_operator(): whole = lax.all_gather(masked, 'row', axis=1, tiled=True)  79.1 us
    all_gather x1, waiting for transfers between devices, local(): col_states = lax.all_gather(states, 'row', axis=0, tiled=True)  68.1 us
    all_gather x1, waiting for transfers between devices, local(): row_states = lax.all_gather(states, 'col', axis=0, tiled=True)  48.7 us
    unnamed x2, matrix products  17.6 us
  transfers between devices with their start and end apart: 4, of which 4 were waited for; matrix products, arithmetic and copies ran while one was open for 0% of the time, Pallas kernels for 0%

commit v1 on v0

v1 whole, which is shorter than its diff:
```python
import math

import jax
import jax.numpy as jnp
from jax import lax
from jax.experimental import pallas as pl
from jax.experimental.pallas import tpu as pltpu
from jax.sharding import PartitionSpec as P

MESH = pl.DeviceIdType.MESH
RING = 8
SAMP = 64
DIM = 512
OUT = 32
ROUNDS = 8
EXP_SCALE = math.log2(math.e) * 2.0 / DIM


def offsets(n, j):
    if n == 0:
        return 0, j
    if n == 7:
        return 4, j
    k, a = (n + 1) // 2, (n - 1) % 2
    return (RING - k if j == 0 else k), a


def mirror(n, j):
    return j if n in (0, 7) else 1 - j


def lane_group():
    return lax.broadcasted_iota(jnp.int32, (16, 128), 1) // OUT


def by_group(pieces):
    group = lane_group()
    out = pieces[3]
    for g in (2, 1, 0):
        out = jnp.where(group == g, pieces[g], out)
    return out


def pack(block, at):
    return by_group(
        [
            pltpu.roll(block[16 * g : 16 * g + 16], (OUT * (g - at)) % 128, axis=1)
            if g != at
            else block[16 * g : 16 * g + 16]
            for g in range(4)
        ]
    )


def fold_lanes(x):
    x = x + pltpu.roll(x, 64, axis=1)
    return x + pltpu.roll(x, 32, axis=1)


def kernel(
    states, targets, start_coef, washout,
    coef_out, res_out,
    col_st, row_st, e_hi, e_lo, w_all, flip,
    vec0, part1, got1, vec1, vec1r, part2, got2, dots, got_dots,
    send_sem, sib_send, c_recv, s_recv, r_recv, v_recv, vs_recv, phase_recv,
):
    row, col = lax.axis_index("row"), lax.axis_index("col")
    core, xl, y = row % 2, (row // 2) % 2, row // 4
    xh, z = col % 2, col // 2

    def row_peer(dy, dxl, dcore):
        return (((y + dy) % RING * 2 + (xl + dxl) % 2) * 2 + (core + dcore) % 2, col)

    def col_peer(dz, dxh):
        return (row, (z + dz) % RING * 2 + (xh + dxh) % 2)

    y_up, y_down = row_peer(1, 0, 0), row_peer(RING - 1, 0, 0)
    z_up, z_down = col_peer(1, 0), col_peer(RING - 1, 0)
    x_near, sibling, x_far = row_peer(0, 1, 0), row_peer(0, 0, 1), col_peer(0, 1)
    near = (y_up, y_down, z_up, z_down, x_near, sibling, x_far)

    barrier = pltpu.get_barrier_semaphore()
    for who in near:
        pl.semaphore_signal(barrier, inc=1, device_id=who, device_id_type=MESH)
    pl.semaphore_wait(barrier, len(near))

    def send(src, dst, to, s_sem, r_sem):
        pltpu.make_async_remote_copy(
            src_ref=src, dst_ref=dst, send_sem=s_sem, recv_sem=r_sem, device_id=to, device_id_type=MESH
        ).start()

    def wait(ref, sem):
        pltpu.make_async_copy(ref, ref, sem).wait()

    def c_slot(n, j):
        return 4 * n + j

    def r_slot(n, j):
        return 2 * n + j

    def send_c(src, n, j, to):
        send(src, col_st.at[c_slot(n, j)], to, send_sem.at[0], c_recv.at[r_slot(n, j)])

    def send_r(src, n, j, to):
        send(src, row_st.at[r_slot(n, j)], to, send_sem.at[1], r_recv.at[r_slot(n, j)])

    def send_v(src, n, j, to):
        send(src, vec0.at[c_slot(n, j)], to, send_sem.at[2], v_recv.at[r_slot(n, j)])

    send_c(states, 1, 0, y_up)
    send_c(states, 1, 1, y_down)
    send_r(states, 1, 0, z_up)
    send_r(states, 1, 1, z_down)
    send_c(states, 0, 1, x_near)
    send_r(states, 0, 1, x_far)
    col_st[0] = states[...]
    row_st[0] = states[...]

    own_f = states[...].astype(jnp.float32)
    norm = jnp.sum(own_f * own_f, axis=1, keepdims=True)
    damp_col = jnp.broadcast_to(jnp.exp(norm * (-1.0 / DIM)), (SAMP, 128))
    damp = by_group([damp_col[16 * g : 16 * g + 16] for g in range(4)])
    flip[...] = jnp.zeros((128, 128), jnp.float32)
    flip[0:OUT, 0:SAMP] = targets[...]
    flip[OUT : 2 * OUT, 0:SAMP] = start_coef[...]
    flip[2 * OUT : 3 * OUT, 0:SAMP] = jnp.broadcast_to(washout[...].astype(jnp.float32), (OUT, SAMP))
    turned = flip[...].T[0:SAMP]
    mask = pack(turned, 2)
    target = pack(turned, 0) * mask
    start = pack(turned, 1)
    scale = mask * damp
    vec0[0] = scale * start

    send_v(vec0.at[0], 1, 0, y_up)
    send_v(vec0.at[0], 1, 1, y_down)
    send_v(vec0.at[0], 0, 1, x_near)

    def pass_on(n):
        if n == 0:
            wait(col_st.at[1], c_recv.at[1])
            send_c(col_st.at[1], 2, 0, y_up)
            send_c(col_st.at[1], 2, 1, y_down)
            wait(row_st.at[1], r_recv.at[1])
            send_r(row_st.at[1], 2, 0, z_up)
            send_r(row_st.at[1], 2, 1, z_down)
            wait(vec0.at[1], v_recv.at[1])
            send_v(vec0.at[1], 2, 0, y_up)
            send_v(vec0.at[1], 2, 1, y_down)
        else:
            for j in (0, 1):
                to_y, to_z = (y_up, z_up) if j == 0 else (y_down, z_down)
                after = n + 2 if n < 5 else 7
                go = n < 5 or (n == 5 and j == 0) or (n == 6 and j == 1)
                wait(col_st.at[c_slot(n, j)], c_recv.at[r_slot(n, j)])
                if go:
                    send_c(col_st.at[c_slot(n, j)], after, j, to_y)
                wait(row_st.at[r_slot(n, j)], r_recv.at[r_slot(n, j)])
                if go:
                    send_r(row_st.at[r_slot(n, j)], after, j, to_z)
                wait(vec0.at[c_slot(n, j)], v_recv.at[r_slot(n, j)])
                if go:
                    send_v(vec0.at[c_slot(n, j)], after, j, to_y)
        own, other = pl.ds(4 * n, 2), pl.ds(4 * n + 2, 2)
        send(col_st.at[own], col_st.at[other], sibling, sib_send.at[0], s_recv.at[n])
        send(vec0.at[own], vec0.at[other], sibling, sib_send.at[1], vs_recv.at[n])

    def block(rows, r_at, columns, c_at, r_count, c_count):
        left = row_st[r_at : r_at + r_count].reshape(r_count * SAMP, DIM)
        right = col_st[c_at : c_at + c_count].reshape(c_count * SAMP, DIM)
        cross = lax.dot_general(left, right, (((1,), (1,)), ((), ())), preferred_element_type=jnp.float32)
        e = jnp.exp2(cross * EXP_SCALE)
        hi = e.astype(jnp.bfloat16)
        e_hi[rows, columns] = hi
        e_lo[rows, columns] = (e - hi.astype(jnp.float32)).astype(jnp.bfloat16)

    def compute(n):
        other = pl.ds(4 * n + 2, 2)
        wait(col_st.at[other], s_recv.at[n])
        columns = pl.ds(256 * n, 256)
        for at in range(n + 1):
            block(pl.ds(128 * at, 128), 2 * at, columns, 4 * n, 2, 4)
        for at in range(n):
            block(pl.ds(128 * n, 128), 2 * n, pl.ds(256 * at, 256), 4 * at, 2, 4)

    for n in range(ROUNDS):
        pass_on(n)
        if n >= 1:
            compute(n - 1)
    compute(ROUNDS - 1)
    for n in range(ROUNDS):
        wait(vec0.at[pl.ds(4 * n + 2, 2)], vs_recv.at[n])

    group = lane_group()

    def spread(vec):
        def one(s, carry):
            v = vec[s, 0:16, :]
            hi = v.astype(jnp.bfloat16).astype(jnp.float32)
            lo = v - hi
            at = pl.multiple_of(s * SAMP, SAMP)
            for g in range(4):
                keep = group == g
                w_all[pl.ds(at + 16 * g, 16), 0:128] = jnp.where(keep, hi, 0.0).astype(jnp.bfloat16)
                w_all[pl.ds(at + 16 * g, 16), 128:256] = jnp.where(keep, lo, 0.0).astype(jnp.bfloat16)
            return carry

        lax.fori_loop(0, 32, one, 0)

    def apply(part):
        for chunk in range(4):
            rows = pl.ds(256 * chunk, 256)
            both = jnp.dot(e_hi[rows, :], w_all[...], preferred_element_type=jnp.float32)
            low = jnp.dot(e_lo[rows, :], w_all[:, 0:128], preferred_element_type=jnp.float32)
            acc = fold_lanes(both[:, 0:128] + both[:, 128:256] + low)
            for s in range(4):
                part[4 * chunk + s, 0:16, :] = by_group(
                    [acc[64 * s + 16 * g : 64 * s + 16 * g + 16] for g in range(4)]
                )

    row_slots = [(n, j) for n in range(ROUNDS) for j in (0, 1)]

    def to_owners(part, got, s_sem, r_sem):
        for n, j in row_slots[1:]:
            dz, dxh = offsets(n, j)
            send(part.at[r_slot(n, j)], got.at[r_slot(n, mirror(n, j))], col_peer(dz, dxh), s_sem, r_sem)

    spread(vec0)
    apply(part1)
    to_owners(part1, got1, send_sem.at[3], phase_recv.at[0])
    wait(got1.at[pl.ds(1, 15)], phase_recv.at[0])
    total = part1[0]
    for s in range(1, 16):
        total = total + got1[s]
    r0 = target - (scale * total + start)
    weight = scale * r0
    squares = jnp.broadcast_to(jnp.sum(r0 * r0, axis=0, keepdims=True), (8, 128))
    vec1[0, 0:16, :] = weight
    vec1[0, 16:24, :] = squares
    vec1r[0] = weight

    for n, j in row_slots:
        dy, dxl = offsets(n, j)
        for dcore in (0, 1):
            if (n, j, dcore) == (0, 0, 0):
                continue
            at = 4 * n + 2 * dcore + mirror(n, j)
            send(vec1.at[0], vec1.at[at], row_peer(dy, dxl, dcore), send_sem.at[4], phase_recv.at[1])
    for n, j in row_slots[1:]:
        dz, dxh = offsets(n, j)
        send(vec1r.at[0], vec1r.at[r_slot(n, mirror(n, j))], col_peer(dz, dxh), send_sem.at[5], phase_recv.at[2])
    wait(vec1.at[pl.ds(1, 31)], phase_recv.at[1])
    spread(vec1)
    apply(part2)
    wait(vec1r.at[pl.ds(1, 15)], phase_recv.at[2])
    bend = vec1r[0] * part2[0, 0:16, :]
    for s in range(1, 16):
        bend = bend + vec1r[s] * part2[s, 0:16, :]
    bend = jnp.sum(bend, axis=0, keepdims=True)
    sq = vec1[0, 16:24, :]
    for s in range(1, 32):
        sq = sq + vec1[s, 16:24, :]
    tail = jnp.where(lax.broadcasted_iota(jnp.int32, (8, 128), 0) == 0, jnp.broadcast_to(bend, (8, 128)), sq)
    for s in range(16):
        part2[s, 16:24, :] = tail
    to_owners(part2, got2, send_sem.at[6], phase_recv.at[3])
    wait(got2.at[pl.ds(1, 15)], phase_recv.at[3])
    total = part2[0]
    for s in range(1, 16):
        total = total + got2[s]
    q = scale * total[0:16] + r0
    tail = total[16:24]
    dots[...] = tail
    for n, j in row_slots:
        dy, dxl = offsets(n, j)
        for dcore in (0, 1):
            if (n, j, dcore) == (0, 0, 0):
                continue
            at = 4 * n + 2 * dcore + mirror(n, j)
            send(dots, got_dots.at[at], row_peer(dy, dxl, dcore), send_sem.at[7], phase_recv.at[4])
    wait(got_dots.at[pl.ds(1, 31)], phase_recv.at[4])
    bend = tail
    for s in range(1, 32):
        bend = bend + got_dots[s]
    squares = fold_lanes(tail)[1:2]
    bend = fold_lanes(bend)[0:1] + squares
    alpha = squares / bend
    coef = start + alpha * r0
    res = r0 - alpha * q
    flip[...] = jnp.zeros((128, 128), jnp.float32)
    low = lax.broadcasted_iota(jnp.int32, (16, 128), 1) < OUT
    for g in range(4):
        a = pltpu.roll(coef, (128 - OUT * g) % 128, axis=1) if g else coef
        b = pltpu.roll(res, (128 + OUT - OUT * g) % 128, axis=1) if g != 1 else res
        flip[16 * g : 16 * g + 16, :] = jnp.where(low, a, b)
    back = flip[...].T
    coef_out[...] = back[0:OUT, 0:SAMP]
    res_out[...] = back[OUT : 2 * OUT, 0:SAMP]

    wait(col_st.at[pl.ds(0, 15)], send_sem.at[0])
    wait(row_st.at[pl.ds(0, 15)], send_sem.at[1])
    wait(vec0.at[pl.ds(0, 15)], send_sem.at[2])
    wait(col_st.at[pl.ds(0, 16)], sib_send.at[0])
    wait(vec0.at[pl.ds(0, 16)], sib_send.at[1])
    wait(part1.at[pl.ds(0, 15)], send_sem.at[3])
    wait(vec1.at[pl.ds(0, 31)], send_sem.at[4])
    wait(vec1r.at[pl.ds(0, 15)], send_sem.at[5])
    wait(part2.at[pl.ds(0, 15)], send_sem.at[6])
    wait(got_dots.at[pl.ds(0, 31)], send_sem.at[7])


def local(states, targets, start_coef, washout):
    f32, bf16 = jnp.float32, jnp.bfloat16
    vmem = pl.BlockSpec(memory_space=pltpu.VMEM)
    out = jax.ShapeDtypeStruct((OUT, SAMP), f32)
    return pl.pallas_call(
        kernel,
        out_shape=(out, out),
        in_specs=[vmem] * 4,
        out_specs=(vmem, vmem),
        scratch_shapes=[
            pltpu.VMEM((32, SAMP, DIM), bf16),
            pltpu.VMEM((16, SAMP, DIM), bf16),
            pltpu.VMEM((1024, 2048), bf16),
            pltpu.VMEM((1024, 2048), bf16),
            pltpu.VMEM((2048, 256), bf16),
            pltpu.VMEM((128, 128), f32),
            pltpu.VMEM((32, 16, 128), f32),
            pltpu.VMEM((16, 16, 128), f32),
            pltpu.VMEM((16, 16, 128), f32),
            pltpu.VMEM((32, 24, 128), f32),
            pltpu.VMEM((16, 16, 128), f32),
            pltpu.VMEM((16, 24, 128), f32),
            pltpu.VMEM((16, 24, 128), f32),
            pltpu.VMEM((8, 128), f32),
            pltpu.VMEM((32, 8, 128), f32),
            pltpu.SemaphoreType.DMA((8,)),
            pltpu.SemaphoreType.DMA((2,)),
            pltpu.SemaphoreType.DMA((16,)),
            pltpu.SemaphoreType.DMA((8,)),
            pltpu.SemaphoreType.DMA((16,)),
            pltpu.SemaphoreType.DMA((16,)),
            pltpu.SemaphoreType.DMA((8,)),
            pltpu.SemaphoreType.DMA((5,)),
        ],
        compiler_params=pltpu.CompilerParams(
            collective_id=0, has_side_effects=True, vmem_limit_bytes=48 * 1024 * 1024
        ),
    )(states, targets, start_coef, washout.reshape(1, SAMP))


def solution(mesh):
    return jax.shard_map(
        local,
        mesh=mesh,
        in_specs=(
            P(("row", "col"), None),
            P(None, ("row", "col")),
            P(None, ("row", "col")),
            P(("row", "col")),
        ),
        out_specs=(P(None, ("row", "col")), P(None, ("row", "col"))),
        check_vma=False,
    )
```

time: 744 us -> 81.6 us (0.11)
  waiting for transfers between devices: 518 us -> 0 us
  blocking collectives: 179 us -> 0 us
  Pallas kernels: 0 us -> 76.1 us
  matrix products: 22.1 us -> 0 us
  between operations: 13.8 us -> 0.65 us
    unnamed x6 -> x0, waiting for transfers between devices: 401 us -> none
    all_gather x2 -> x0, waiting for transfers between devices: 117 us -> none  [the longest x1 68.1 us: local(): col_states = lax.all_gather(states, 'row', axis=0, tiled=True)]
    psum x1 -> x0, blocking collectives: 100 us -> none  [local(): squares = lax.psum(local_squares, ('row', 'col'))]
    all_gather x2 -> x0, blocking collectives: 79.1 us -> none  [apply_operator(): whole = lax.all_gather(masked, 'row', axis=1, tiled=True)]
    pallas_call x0 -> x1, Pallas kernels: none -> 76.1 us  [local(): pl.pallas_call(kernel, out_shape=(out, out), in_specs=[vmem] * 4, out_spe...]
    unnamed x2 -> x0, matrix products: 17.6 us -> none
  transfers between devices with their start and end apart: 4 -> 0, of which waited for: 4 -> 0; matrix products, arithmetic and copies ran while one was open for 0% -> 0% of each run, Pallas kernels for 0% -> 0%
where the time goes in v1:
time: 81.6 us; the launch traced here: 80.8 us
  Pallas kernels  76.1 us (93%)
  local copies, waits for them, and re-layouts  4.13 us (5%)
    pallas_call x1, Pallas kernels, local(): pl.pallas_call(kernel, out_shape=(out, out), in_specs=[vmem] * 4, out_spe...  76.1 us
    unnamed x10, local copies, waits for them, and re-layouts  4.13 us

profile of v1, /device:TPU:1, one launch (start us, length us, event | category | flops | bytes accessed | tf_op | source)
XLA Modules:
  0.0 80.8 jit_solution(2998742814634111322)
XLA Ops:
  0.6 0.0 copy-start.3
  0.6 0.6 copy-done.3
  1.3 0.0 copy-start
  1.3 0.8 %copy-done = bf16[64,512]{1,0:T(8,128)(2,1)S(1)} copy-done((bf16[64,512]{1,0:T(8,128)(2,1)S(1)}, bf16[64,512]{1,0:T(8,128)(2,1)}, u32[]{:S(2)}) %copy-start) | copy-done | bytes 65560
  2.1 0.0 copy-start.1
  2.1 0.7 copy-done.1
  2.8 0.0 copy-start.2
  2.8 0.7 copy-done.2
  3.6 76.1 %shard_map.59 = (f32[32,64]{1,0:T(8,128)S(1)}, f32[32,64]{1,0:T(8,128)S(1)}) custom-call(bf16[64,512]{1,0:T(8,128)(2,1)S(1)} %copy-done, f32[32,64]{1,0:T(8,128)S(1)} %copy-done.1, f32[32,64]{1,0:T(8,128)S(1)} %copy-done.2, s32[1,64]{1,0:T(1,128)S(1)} %bitcast.1), custom_call_target="tpu_custom_call" | custom-call | tf_op jit(solution)/shard_map/pallas_call | solution.py:315
  79.6 0.6 copy.8
  80.2 0.6 copy.9
Async XLA Ops:
  0.6 0.7 copy-start.3
  1.3 0.8 %copy-start = (bf16[64,512]{1,0:T(8,128)(2,1)S(1)}, bf16[64,512]{1,0:T(8,128)(2,1)}, u32[]{:S(2)}) copy-start(bf16[64,512]{1,0:T(8,128)(2,1)} %states.1) | copy-start | bytes 196612
  2.1 0.7 copy-start.1
  2.8 0.7 copy-start.2

commit v2 on v1

v2 whole, which is shorter than its diff:
```python
import math

import jax
import jax.numpy as jnp
from jax import lax
from jax.experimental import pallas as pl
from jax.experimental.pallas import tpu as pltpu
from jax.sharding import PartitionSpec as P

MESH = pl.DeviceIdType.MESH
RING = 8
SAMP = 64
DIM = 512
OUT = 32
ROUNDS = 8
EXP_SCALE = math.log2(math.e) * 2.0 / DIM


def offsets(n, j):
    if n == 0:
        return 0, j
    if n == 7:
        return 4, j
    k, a = (n + 1) // 2, (n - 1) % 2
    return (RING - k if j == 0 else k), a


def mirror(n, j):
    return j if n in (0, 7) else 1 - j


def lane_group():
    return lax.broadcasted_iota(jnp.int32, (16, 128), 1) // OUT


def by_group(pieces):
    group = lane_group()
    out = pieces[3]
    for g in (2, 1, 0):
        out = jnp.where(group == g, pieces[g], out)
    return out


def pack(block, at):
    return by_group(
        [
            pltpu.roll(block[16 * g : 16 * g + 16], (OUT * (g - at)) % 128, axis=1)
            if g != at
            else block[16 * g : 16 * g + 16]
            for g in range(4)
        ]
    )


def fold_lanes(x):
    x = x + pltpu.roll(x, 64, axis=1)
    return x + pltpu.roll(x, 32, axis=1)


def kernel(
    states_in, targets_in, coef_in, washout_in,
    coef_out, res_out,
    states, vectors, washout, col_st, row_st, e_hi, e_lo, w_all, acc, flip,
    vec0, part1, got1, vec1, vec1r, part2, got2, dots, got_dots, got_dots2,
    in_sem, send_sem, sib_send, c_recv, s_recv, r_recv, v_recv, vs_recv, phase_recv,
):
    row, col = lax.axis_index("row"), lax.axis_index("col")
    core, xl, y = row % 2, (row // 2) % 2, row // 4
    xh, z = col % 2, col // 2

    def row_peer(dy, dxl, dcore):
        return (((y + dy) % RING * 2 + (xl + dxl) % 2) * 2 + (core + dcore) % 2, col)

    def col_peer(dz, dxh):
        return (row, (z + dz) % RING * 2 + (xh + dxh) % 2)

    y_up, y_down = row_peer(1, 0, 0), row_peer(RING - 1, 0, 0)
    z_up, z_down = col_peer(1, 0), col_peer(RING - 1, 0)
    x_near, sibling, x_far = row_peer(0, 1, 0), row_peer(0, 0, 1), col_peer(0, 1)
    near = (y_up, y_down, z_up, z_down, x_near, sibling, x_far)

    barrier = pltpu.get_barrier_semaphore()
    for who in near:
        pl.semaphore_signal(barrier, inc=1, device_id=who, device_id_type=MESH)

    fetches = [
        pltpu.make_async_copy(states_in, states, in_sem.at[0]),
        pltpu.make_async_copy(targets_in, vectors.at[0], in_sem.at[1]),
        pltpu.make_async_copy(coef_in, vectors.at[1], in_sem.at[2]),
        pltpu.make_async_copy(washout_in, washout, in_sem.at[3]),
    ]
    for fetch in fetches:
        fetch.start()
    fetches[0].wait()
    pl.semaphore_wait(barrier, len(near))

    def send(src, dst, to, s_sem, r_sem):
        pltpu.make_async_remote_copy(
            src_ref=src, dst_ref=dst, send_sem=s_sem, recv_sem=r_sem, device_id=to, device_id_type=MESH
        ).start()

    def wait(ref, sem):
        pltpu.make_async_copy(ref, ref, sem).wait()

    def slot(n, j):
        return 2 * n + j

    def send_c(src, n, j, to):
        send(src, col_st.at[slot(n, j)], to, send_sem.at[0], c_recv.at[slot(n, j)])

    def send_r(src, n, j, to):
        send(src, row_st.at[slot(n, j)], to, send_sem.at[1], r_recv.at[slot(n, j)])

    def send_v(src, n, j, to):
        send(src, vec0.at[slot(n, j)], to, send_sem.at[2], v_recv.at[slot(n, j)])

    send_c(states, 1, 0, y_up)
    send_c(states, 1, 1, y_down)
    send_r(states, 1, 0, z_up)
    send_r(states, 1, 1, z_down)
    send_r(states, 0, 1, x_far)
    send_c(states, 0, 1, x_near)
    col_st[0] = states[...]
    row_st[0] = states[...]

    own_f = states[...].astype(jnp.float32)
    norm = jnp.sum(own_f * own_f, axis=1, keepdims=True)
    damp_col = jnp.broadcast_to(jnp.exp(norm * (-1.0 / DIM)), (SAMP, 128))
    damp = by_group([damp_col[16 * g : 16 * g + 16] for g in range(4)])
    for fetch in fetches[1:]:
        fetch.wait()
    flip[0:OUT, 0:SAMP] = vectors[0]
    flip[OUT : 2 * OUT, 0:SAMP] = vectors[1]
    flip[2 * OUT : 3 * OUT, 0:SAMP] = jnp.broadcast_to(washout[...].astype(jnp.float32), (OUT, SAMP))
    turned = flip[...].T[0:SAMP]
    mask = pack(turned, 2)
    target = pack(turned, 0) * mask
    start = pack(turned, 1)
    scale = mask * damp
    vec0[0] = scale * start

    send_v(vec0.at[0], 1, 0, y_up)
    send_v(vec0.at[0], 1, 1, y_down)
    send_v(vec0.at[0], 0, 1, x_near)

    def pass_states(n):
        if n == 0:
            wait(row_st.at[1], r_recv.at[1])
            send_r(row_st.at[1], 2, 0, z_up)
            send_r(row_st.at[1], 2, 1, z_down)
            wait(col_st.at[1], c_recv.at[1])
            send_c(col_st.at[1], 2, 0, y_up)
            send_c(col_st.at[1], 2, 1, y_down)
        else:
            for j in (0, 1):
                to_y, to_z = (y_up, z_up) if j == 0 else (y_down, z_down)
                after = n + 2 if n < 5 else 7
                go = n < 5 or (n == 5 and j == 0) or (n == 6 and j == 1)
                wait(row_st.at[slot(n, j)], r_recv.at[slot(n, j)])
                if go:
                    send_r(row_st.at[slot(n, j)], after, j, to_z)
                wait(col_st.at[slot(n, j)], c_recv.at[slot(n, j)])
                if go:
                    send_c(col_st.at[slot(n, j)], after, j, to_y)
        send(
            col_st.at[pl.ds(2 * n, 2)], col_st.at[pl.ds(16 + 2 * n, 2)], sibling, sib_send.at[0], s_recv.at[n]
        )

    def pass_vectors(n):
        if n == 0:
            wait(vec0.at[1], v_recv.at[1])
            send_v(vec0.at[1], 2, 0, y_up)
            send_v(vec0.at[1], 2, 1, y_down)
        else:
            for j in (0, 1):
                to_y = y_up if j == 0 else y_down
                after = n + 2 if n < 5 else 7
                go = n < 5 or (n == 5 and j == 0) or (n == 6 and j == 1)
                wait(vec0.at[slot(n, j)], v_recv.at[slot(n, j)])
                if go:
                    send_v(vec0.at[slot(n, j)], after, j, to_y)
        send(vec0.at[pl.ds(2 * n, 2)], vec0.at[pl.ds(16 + 2 * n, 2)], sibling, sib_send.at[1], vs_recv.at[n])

    group = lane_group()

    def spread(vec, first, count):
        for s in range(first, first + count):
            v = vec[s]
            hi = v.astype(jnp.bfloat16).astype(jnp.float32)
            lo = v - hi
            for g in range(4):
                keep = group == g
                at = SAMP * s + 16 * g
                w_all[at : at + 16, 0:128] = jnp.where(keep, hi, 0.0).astype(jnp.bfloat16)
                w_all[at : at + 16, 128:256] = jnp.where(keep, lo, 0.0).astype(jnp.bfloat16)

    def product(hi, lo, w):
        both = jnp.dot(hi, w, preferred_element_type=jnp.float32)
        low = jnp.dot(lo, w[:, 0:128], preferred_element_type=jnp.float32)
        return both[:, 0:128] + both[:, 128:256] + low

    def tile(r_first, r_count, ranges, fresh):
        left = row_st[r_first : r_first + r_count].reshape(r_count * SAMP, DIM)
        right = jnp.concatenate([col_st[a : a + k].reshape(k * SAMP, DIM) for a, k in ranges], axis=0)
        w = jnp.concatenate([w_all[a * SAMP : (a + k) * SAMP] for a, k in ranges], axis=0)
        cross = lax.dot_general(left, right, (((1,), (1,)), ((), ())), preferred_element_type=jnp.float32)
        e = jnp.exp2(cross * EXP_SCALE)
        hi = e.astype(jnp.bfloat16)
        lo = (e - hi.astype(jnp.float32)).astype(jnp.bfloat16)
        rows = pl.ds(r_first * SAMP, r_count * SAMP)
        at = 0
        for a, k in ranges:
            columns = pl.ds(a * SAMP, k * SAMP)
            e_hi[rows, columns] = hi[:, at : at + k * SAMP]
            e_lo[rows, columns] = lo[:, at : at + k * SAMP]
            at += k * SAMP
        add = product(hi, lo, w)
        acc[rows, :] = add if fresh else acc[rows, :] + add

    def compute(n, rounds):
        for k in range(n, n + rounds):
            wait(col_st.at[pl.ds(16 + 2 * k, 2)], s_recv.at[k])
            wait(vec0.at[pl.ds(16 + 2 * k, 2)], vs_recv.at[k])
        spread(vec0, 2 * n, 2 * rounds)
        spread(vec0, 16 + 2 * n, 2 * rounds)
        new = [(2 * n, 2 * rounds), (16 + 2 * n, 2 * rounds)]
        if n:
            tile(0, 2 * n, new, False)
            tile(2 * n, 2 * rounds, [(0, 2 * n + 2 * rounds), (16, 2 * n + 2 * rounds)], True)
        else:
            tile(0, 2 * rounds, new, True)

    pass_states(0)
    pass_states(1)
    pass_vectors(0)
    pass_vectors(1)
    compute(0, 2)
    pass_states(2)
    pass_states(3)
    pass_vectors(2)
    pass_vectors(3)
    compute(2, 2)
    pass_states(4)
    pass_states(5)
    pass_vectors(4)
    pass_vectors(5)
    compute(4, 2)
    pass_states(6)
    pass_vectors(6)
    compute(6, 1)
    pass_states(7)
    pass_vectors(7)
    compute(7, 1)

    row_slots = [(n, j) for n in range(ROUNDS) for j in (0, 1)]
    far_first = row_slots[::-1]

    def to_owner(part, got, n, j, s_sem, r_sem):
        s = slot(n, j)
        whole = fold_lanes(acc[SAMP * s : SAMP * s + SAMP, :])
        part[s] = by_group([whole[16 * g : 16 * g + 16] for g in range(4)])
        if s:
            dz, dxh = offsets(n, j)
            send(part.at[s], got.at[slot(n, mirror(n, j))], col_peer(dz, dxh), s_sem, r_sem)

    for n, j in far_first:
        to_owner(part1, got1, n, j, send_sem.at[3], phase_recv.at[0])
    wait(got1.at[pl.ds(1, 15)], phase_recv.at[0])
    total = part1[0]
    for s in range(1, 16):
        total = total + got1[s]
    r0 = target - (scale * total + start)
    weight = scale * r0
    vec1[0] = weight
    vec1r[0] = weight

    for n, j in far_first[:-1]:
        dy, dxl = offsets(n, j)
        at = slot(n, mirror(n, j))
        send(vec1.at[0], vec1.at[at], row_peer(dy, dxl, 0), send_sem.at[4], phase_recv.at[1 if n < 4 else 2])
    send(vec1.at[0], vec1.at[16], sibling, sib_send.at[2], phase_recv.at[3])
    for n, j in far_first[:-1]:
        dz, dxh = offsets(n, j)
        send(vec1r.at[0], vec1r.at[slot(n, mirror(n, j))], col_peer(dz, dxh), send_sem.at[5], phase_recv.at[6])

    def second(first, count, fresh, rows):
        columns = pl.ds(first * SAMP, count * SAMP)
        add = product(e_hi[rows, columns], e_lo[rows, columns], w_all[columns, :])
        acc[rows, :] = add if fresh else acc[rows, :] + add

    every = pl.ds(0, 1024)
    wait(vec1.at[pl.ds(1, 7)], phase_recv.at[1])
    send(vec1.at[pl.ds(1, 7)], vec1.at[pl.ds(17, 7)], sibling, sib_send.at[2], phase_recv.at[4])
    spread(vec1, 0, 8)
    second(0, 8, True, every)
    wait(vec1.at[pl.ds(8, 8)], phase_recv.at[2])
    send(vec1.at[pl.ds(8, 8)], vec1.at[pl.ds(24, 8)], sibling, sib_send.at[2], phase_recv.at[5])
    spread(vec1, 8, 8)
    second(8, 8, False, every)
    wait(vec1.at[16], phase_recv.at[3])
    wait(vec1.at[pl.ds(17, 7)], phase_recv.at[4])
    spread(vec1, 16, 8)
    second(16, 8, False, every)
    wait(vec1.at[pl.ds(24, 8)], phase_recv.at[5])
    spread(vec1, 24, 8)
    for chunk in (3, 2, 1, 0):
        second(24, 8, False, pl.ds(256 * chunk, 256))
        for n, j in far_first[12 - 4 * chunk : 16 - 4 * chunk]:
            to_owner(part2, got2, n, j, send_sem.at[6], phase_recv.at[7])

    wait(vec1r.at[pl.ds(1, 15)], phase_recv.at[6])
    bend = vec1r[0] * part2[0]
    for s in range(1, 16):
        bend = bend + vec1r[s] * part2[s]
    bend = jnp.sum(bend, axis=0, keepdims=True)
    squares = jnp.sum(r0 * r0, axis=0, keepdims=True)
    first_row = lax.broadcasted_iota(jnp.int32, (8, 128), 0) == 0
    both = fold_lanes(jnp.where(first_row, jnp.broadcast_to(bend, (8, 128)), jnp.broadcast_to(squares, (8, 128))))
    dots[0] = both
    two = pl.ds(0, 2)
    for n, j in far_first:
        dy, dxl = offsets(n, j)
        for dcore in (1, 0):
            if (n, j, dcore) != (0, 0, 0):
                at = 16 * dcore + slot(n, mirror(n, j))
                send(
                    dots.at[0, two], got_dots.at[at, two], row_peer(dy, dxl, dcore), send_sem.at[7], phase_recv.at[8]
                )
    wait(got_dots.at[pl.ds(1, 31), two], phase_recv.at[8])
    both = both[0:2]
    for s in range(1, 32):
        both = both + got_dots[s, 0:2, :]
    dots[1, 0:2, :] = both
    for n, j in far_first[:-1]:
        dz, dxh = offsets(n, j)
        at = slot(n, mirror(n, j))
        send(dots.at[1, two], got_dots2.at[at, two], col_peer(dz, dxh), send_sem.at[8], phase_recv.at[9])
    wait(got2.at[pl.ds(1, 15)], phase_recv.at[7])
    total = part2[0]
    for s in range(1, 16):
        total = total + got2[s]
    q = scale * total + r0
    wait(got_dots2.at[pl.ds(1, 15), two], phase_recv.at[9])
    for s in range(1, 16):
        both = both + got_dots2[s, 0:2, :]
    squares = both[1:2]
    alpha = squares / (both[0:1] + squares)
    coef = start + alpha * r0
    res = r0 - alpha * q
    low = lax.broadcasted_iota(jnp.int32, (16, 128), 1) < OUT
    for g in range(4):
        a = pltpu.roll(coef, (128 - OUT * g) % 128, axis=1) if g else coef
        b = pltpu.roll(res, (128 + OUT - OUT * g) % 128, axis=1) if g != 1 else res
        flip[16 * g : 16 * g + 16, :] = jnp.where(low, a, b)
    back = flip[...].T
    coef_out[...] = back[0:OUT, 0:SAMP]
    res_out[...] = back[OUT : 2 * OUT, 0:SAMP]

    wait(col_st.at[pl.ds(0, 15)], send_sem.at[0])
    wait(row_st.at[pl.ds(0, 15)], send_sem.at[1])
    wait(vec0.at[pl.ds(0, 15)], send_sem.at[2])
    wait(col_st.at[pl.ds(0, 16)], sib_send.at[0])
    wait(vec0.at[pl.ds(0, 16)], sib_send.at[1])
    wait(vec1.at[pl.ds(0, 16)], sib_send.at[2])
    wait(part1.at[pl.ds(0, 15)], send_sem.at[3])
    wait(vec1.at[pl.ds(0, 15)], send_sem.at[4])
    wait(vec1r.at[pl.ds(0, 15)], send_sem.at[5])
    wait(part2.at[pl.ds(0, 15)], send_sem.at[6])
    wait(got_dots.at[pl.ds(0, 31), two], send_sem.at[7])
    wait(got_dots2.at[pl.ds(0, 15), two], send_sem.at[8])


def local(states, targets, start_coef, washout):
    f32, bf16 = jnp.float32, jnp.bfloat16
    vmem = pl.BlockSpec(memory_space=pltpu.VMEM)
    hbm = pl.BlockSpec(memory_space=pltpu.HBM)
    out = jax.ShapeDtypeStruct((OUT, SAMP), f32)
    dma = pltpu.SemaphoreType.DMA
    return pl.pallas_call(
        kernel,
        out_shape=(out, out),
        in_specs=[hbm] * 4,
        out_specs=(vmem, vmem),
        scratch_shapes=[
            pltpu.VMEM((SAMP, DIM), bf16),
            pltpu.VMEM((2, OUT, SAMP), f32),
            pltpu.VMEM((1, SAMP), jnp.int32),
            pltpu.VMEM((32, SAMP, DIM), bf16),
            pltpu.VMEM((16, SAMP, DIM), bf16),
            pltpu.VMEM((1024, 2048), bf16),
            pltpu.VMEM((1024, 2048), bf16),
            pltpu.VMEM((2048, 256), bf16),
            pltpu.VMEM((1024, 128), f32),
            pltpu.VMEM((128, 128), f32),
            pltpu.VMEM((32, 16, 128), f32),
            pltpu.VMEM((16, 16, 128), f32),
            pltpu.VMEM((16, 16, 128), f32),
            pltpu.VMEM((32, 16, 128), f32),
            pltpu.VMEM((16, 16, 128), f32),
            pltpu.VMEM((16, 16, 128), f32),
            pltpu.VMEM((16, 16, 128), f32),
            pltpu.VMEM((2, 8, 128), f32),
            pltpu.VMEM((32, 8, 128), f32),
            pltpu.VMEM((16, 8, 128), f32),
            dma((4,)),
            dma((9,)),
            dma((3,)),
            dma((16,)),
            dma((8,)),
            dma((16,)),
            dma((16,)),
            dma((8,)),
            dma((10,)),
        ],
        compiler_params=pltpu.CompilerParams(
            collective_id=0, has_side_effects=True, vmem_limit_bytes=48 * 1024 * 1024
        ),
    )(states, targets, start_coef, washout.reshape(1, SAMP))


def solution(mesh):
    return jax.shard_map(
        local,
        mesh=mesh,
        in_specs=(
            P(("row", "col"), None),
            P(None, ("row", "col")),
            P(None, ("row", "col")),
            P(("row", "col")),
        ),
        out_specs=(P(None, ("row", "col")), P(None, ("row", "col"))),
        check_vma=False,
    )
```

time: 81.6 us -> 69.1 us (0.85)
  Pallas kernels: 76.1 us -> 64 us
    pallas_call x1, Pallas kernels: 76.1 us -> 64 us  [local(): pl.pallas_call(kernel, out_shape=(out, out), in_specs=[hbm] * 4, out_spec...]
where the time goes in v2:
time: 69.1 us; the launch traced here: 68.8 us
  Pallas kernels  64 us (93%)
  local copies, waits for them, and re-layouts  4.13 us (6%)
    pallas_call x1, Pallas kernels, local(): pl.pallas_call(kernel, out_shape=(out, out), in_specs=[hbm] * 4, out_spec...  64 us
    unnamed x10, local copies, waits for them, and re-layouts  4.13 us

profile of v2, /device:TPU:1, one launch (start us, length us, event | category | flops | bytes accessed | tf_op | source)
XLA Modules:
  0.0 68.8 jit_solution(16271797306627890815)
XLA Ops:
  0.6 0.0 copy-start.3
  0.6 0.6 copy-done.3
  1.3 0.0 copy-start
  1.3 0.8 %copy-done = bf16[64,512]{1,0:T(8,128)(2,1)S(1)} copy-done((bf16[64,512]{1,0:T(8,128)(2,1)S(1)}, bf16[64,512]{1,0:T(8,128)(2,1)}, u32[]{:S(2)}) %copy-start) | copy-done | bytes 65560
  2.1 0.0 copy-start.1
  2.1 0.7 %copy-done.1 = f32[32,64]{1,0:T(8,128)S(1)} copy-done((f32[32,64]{1,0:T(8,128)S(1)}, f32[32,64]{1,0:T(8,128)}, u32[]{:S(2)}) %copy-start.1) | copy-done | bytes 8216
  2.8 0.0 copy-start.2
  2.8 0.7 %copy-done.2 = f32[32,64]{1,0:T(8,128)S(1)} copy-done((f32[32,64]{1,0:T(8,128)S(1)}, f32[32,64]{1,0:T(8,128)}, u32[]{:S(2)}) %copy-start.2) | copy-done | bytes 8216
  3.6 64.0 %shard_map.59 = (f32[32,64]{1,0:T(8,128)S(1)}, f32[32,64]{1,0:T(8,128)S(1)}) custom-call(bf16[64,512]{1,0:T(8,128)(2,1)S(1)} %copy-done, f32[32,64]{1,0:T(8,128)S(1)} %copy-done.1, f32[32,64]{1,0:T(8,128)S(1)} %copy-done.2, s32[1,64]{1,0:T(1,128)S(1)} %bitcast.1), custom_call_target="tpu_custom_call" | custom-call | tf_op jit(solution)/shard_map/pallas_call | solution.py:379
  67.5 0.6 copy.8
  68.2 0.6 copy.9
Async XLA Ops:
  0.6 0.7 copy-start.3
  1.3 0.8 %copy-start = (bf16[64,512]{1,0:T(8,128)(2,1)S(1)}, bf16[64,512]{1,0:T(8,128)(2,1)}, u32[]{:S(2)}) copy-start(bf16[64,512]{1,0:T(8,128)(2,1)} %states_in.1) | copy-start | bytes 196612
  2.1 0.7 %copy-start.1 = (f32[32,64]{1,0:T(8,128)S(1)}, f32[32,64]{1,0:T(8,128)}, u32[]{:S(2)}) copy-start(f32[32,64]{1,0:T(8,128)} %targets_in.1) | copy-start | bytes 24580
  2.8 0.7 %copy-start.2 = (f32[32,64]{1,0:T(8,128)S(1)}, f32[32,64]{1,0:T(8,128)}, u32[]{:S(2)}) copy-start(f32[32,64]{1,0:T(8,128)} %coef_in.1) | copy-start | bytes 24580

commit v3 on v2

--- a/solution.py
+++ b/solution.py
@@ -12,21 +12,27 @@
 SAMP = 64
 DIM = 512
 OUT = 32
-ROUNDS = 8
+SLOTS = [
+    (0, 0), (0, 1), (-2, 0), (2, 0),
+    (-1, 0), (1, 0), (-2, 1), (2, 1),
+    (-3, 0), (3, 0), (-1, 1), (1, 1),
+    (-3, 1), (3, 1), (4, 0), (4, 1),
+]
+INDEX = {slot: at for at, slot in enumerate(SLOTS)}
+GROUPS = [(0, 4), (4, 4), (8, 4), (12, 2), (14, 2)]
 EXP_SCALE = math.log2(math.e) * 2.0 / DIM
 
 
-def offsets(n, j):
-    if n == 0:
-        return 0, j
-    if n == 7:
-        return 4, j
-    k, a = (n + 1) // 2, (n - 1) % 2
-    return (RING - k if j == 0 else k), a
-
-
-def mirror(n, j):
-    return j if n in (0, 7) else 1 - j
+def place(d, a):
+    return INDEX[(d + RING // 2 - 1) % RING - RING // 2 + 1, a % 2]
+
+
+def mirror(s):
+    return place(-SLOTS[s][0], SLOTS[s][1])
+
+
+def far_first(pair_hops):
+    return sorted(range(1, 16), key=lambda s: -abs(SLOTS[s][0]) - pair_hops * SLOTS[s][1])
 
 
 def lane_group():
@@ -69,15 +75,15 @@
     xh, z = col % 2, col // 2
 
     def row_peer(dy, dxl, dcore):
-        return (((y + dy) % RING * 2 + (xl + dxl) % 2) * 2 + (core + dcore) % 2, col)
+        return (((y + dy + RING) % RING * 2 + (xl + dxl) % 2) * 2 + (core + dcore) % 2, col)
 
     def col_peer(dz, dxh):
-        return (row, (z + dz) % RING * 2 + (xh + dxh) % 2)
-
-    y_up, y_down = row_peer(1, 0, 0), row_peer(RING - 1, 0, 0)
-    z_up, z_down = col_peer(1, 0), col_peer(RING - 1, 0)
-    x_near, sibling, x_far = row_peer(0, 1, 0), row_peer(0, 0, 1), col_peer(0, 1)
-    near = (y_up, y_down, z_up, z_down, x_near, sibling, x_far)
+        return (row, (z + dz + RING) % RING * 2 + (xh + dxh) % 2)
+
+    sibling = row_peer(0, 0, 1)
+    near = [row_peer(1, 0, 0), row_peer(-1, 0, 0), row_peer(0, 1, 0), sibling]
+    near += [col_peer(1, 0), col_peer(-1, 0), col_peer(0, 1)]
+    near += [row_peer(2, 0, 0), row_peer(-2, 0, 0), col_peer(2, 0), col_peer(-2, 0)]
 
     barrier = pltpu.get_barrier_semaphore()
     for who in near:
@@ -102,24 +108,38 @@
     def wait(ref, sem):
         pltpu.make_async_copy(ref, ref, sem).wait()
 
-    def slot(n, j):
-        return 2 * n + j
-
-    def send_c(src, n, j, to):
-        send(src, col_st.at[slot(n, j)], to, send_sem.at[0], c_recv.at[slot(n, j)])
-
-    def send_r(src, n, j, to):
-        send(src, row_st.at[slot(n, j)], to, send_sem.at[1], r_recv.at[slot(n, j)])
-
-    def send_v(src, n, j, to):
-        send(src, vec0.at[slot(n, j)], to, send_sem.at[2], v_recv.at[slot(n, j)])
-
-    send_c(states, 1, 0, y_up)
-    send_c(states, 1, 1, y_down)
-    send_r(states, 1, 0, z_up)
-    send_r(states, 1, 1, z_down)
-    send_r(states, 0, 1, x_far)
-    send_c(states, 0, 1, x_near)
+    def hop(s, d, a=0, half=None):
+        to = place(SLOTS[s][0] - d, SLOTS[s][1] + a)
+        rows = pl.ds(0, SAMP) if half is None else pl.ds(half * 32, 32)
+        sem = to if half is None or half == 0 else 16 + SLOTS[to][1]
+        for buf, peer, k, recv in ((row_st, col_peer(d, a), 1, r_recv), (col_st, row_peer(d, a, 0), 0, c_recv)):
+            src = buf.at[s, rows] if s else states
+            send(src, buf.at[to, rows], peer, send_sem.at[k], recv.at[sem])
+
+    def hop_vector(s, d, a=0):
+        to = place(SLOTS[s][0] - d, SLOTS[s][1] + a)
+        send(vec0.at[s], vec0.at[to], row_peer(d, a, 0), send_sem.at[2], v_recv.at[to])
+
+    def take(s):
+        for buf, recv in ((row_st, r_recv), (col_st, c_recv)):
+            if SLOTS[s][0] == 4:
+                wait(buf.at[s, pl.ds(0, 32)], recv.at[s])
+                wait(buf.at[s, pl.ds(32, 32)], recv.at[16 + SLOTS[s][1]])
+            else:
+                wait(buf.at[s], recv.at[s])
+
+    def take_vector(s):
+        wait(vec0.at[s], v_recv.at[s])
+
+    def share(g):
+        first, count = GROUPS[g]
+        own, other = pl.ds(first, count), pl.ds(16 + first, count)
+        send(col_st.at[own], col_st.at[other], sibling, sib_send.at[0], s_recv.at[g])
+        send(vec0.at[own], vec0.at[other], sibling, sib_send.at[1], vs_recv.at[g])
+
+    hop(0, 0, 1)
+    hop(0, 2)
+    hop(0, -2)
     col_st[0] = states[...]
     row_st[0] = states[...]
 
@@ -139,47 +159,9 @@
     scale = mask * damp
     vec0[0] = scale * start
 
-    send_v(vec0.at[0], 1, 0, y_up)
-    send_v(vec0.at[0], 1, 1, y_down)
-    send_v(vec0.at[0], 0, 1, x_near)
-
-    def pass_states(n):
-        if n == 0:
-            wait(row_st.at[1], r_recv.at[1])
-            send_r(row_st.at[1], 2, 0, z_up)
-            send_r(row_st.at[1], 2, 1, z_down)
-            wait(col_st.at[1], c_recv.at[1])
-            send_c(col_st.at[1], 2, 0, y_up)
-            send_c(col_st.at[1], 2, 1, y_down)
-        else:
-            for j in (0, 1):
-                to_y, to_z = (y_up, z_up) if j == 0 else (y_down, z_down)
-                after = n + 2 if n < 5 else 7
-                go = n < 5 or (n == 5 and j == 0) or (n == 6 and j == 1)
-                wait(row_st.at[slot(n, j)], r_recv.at[slot(n, j)])
-                if go:
-                    send_r(row_st.at[slot(n, j)], after, j, to_z)
-                wait(col_st.at[slot(n, j)], c_recv.at[slot(n, j)])
-                if go:
-                    send_c(col_st.at[slot(n, j)], after, j, to_y)
-        send(
-            col_st.at[pl.ds(2 * n, 2)], col_st.at[pl.ds(16 + 2 * n, 2)], sibling, sib_send.at[0], s_recv.at[n]
-        )
-
-    def pass_vectors(n):
-        if n == 0:
-            wait(vec0.at[1], v_recv.at[1])
-            send_v(vec0.at[1], 2, 0, y_up)
-            send_v(vec0.at[1], 2, 1, y_down)
-        else:
-            for j in (0, 1):
-                to_y = y_up if j == 0 else y_down
-                after = n + 2 if n < 5 else 7
-                go = n < 5 or (n == 5 and j == 0) or (n == 6 and j == 1)
-                wait(vec0.at[slot(n, j)], v_recv.at[slot(n, j)])
-                if go:
-                    send_v(vec0.at[slot(n, j)], after, j, to_y)
-        send(vec0.at[pl.ds(2 * n, 2)], vec0.at[pl.ds(16 + 2 * n, 2)], sibling, sib_send.at[1], vs_recv.at[n])
+    hop_vector(0, 0, 1)
+    hop_vector(0, 2)
+    hop_vector(0, -2)
 
     group = lane_group()
 
@@ -217,54 +199,85 @@
         add = product(hi, lo, w)
         acc[rows, :] = add if fresh else acc[rows, :] + add
 
-    def compute(n, rounds):
-        for k in range(n, n + rounds):
-            wait(col_st.at[pl.ds(16 + 2 * k, 2)], s_recv.at[k])
-            wait(vec0.at[pl.ds(16 + 2 * k, 2)], vs_recv.at[k])
-        spread(vec0, 2 * n, 2 * rounds)
-        spread(vec0, 16 + 2 * n, 2 * rounds)
-        new = [(2 * n, 2 * rounds), (16 + 2 * n, 2 * rounds)]
-        if n:
-            tile(0, 2 * n, new, False)
-            tile(2 * n, 2 * rounds, [(0, 2 * n + 2 * rounds), (16, 2 * n + 2 * rounds)], True)
-        else:
-            tile(0, 2 * rounds, new, True)
-
-    pass_states(0)
-    pass_states(1)
-    pass_vectors(0)
-    pass_vectors(1)
-    compute(0, 2)
-    pass_states(2)
-    pass_states(3)
-    pass_vectors(2)
-    pass_vectors(3)
-    compute(2, 2)
-    pass_states(4)
-    pass_states(5)
-    pass_vectors(4)
-    pass_vectors(5)
-    compute(4, 2)
-    pass_states(6)
-    pass_vectors(6)
-    compute(6, 1)
-    pass_states(7)
-    pass_vectors(7)
-    compute(7, 1)
-
-    row_slots = [(n, j) for n in range(ROUNDS) for j in (0, 1)]
-    far_first = row_slots[::-1]
-
-    def to_owner(part, got, n, j, s_sem, r_sem):
-        s = slot(n, j)
+    def compute(g):
+        first, count = GROUPS[g]
+        spread(vec0, first, count)
+        if first:
+            tile(first, count, [(0, first), (16, first)], True)
+        tile(0, first + count, [(first, count)], first == 0)
+        wait(col_st.at[pl.ds(16 + first, count)], s_recv.at[g])
+        wait(vec0.at[pl.ds(16 + first, count)], vs_recv.at[g])
+        spread(vec0, 16 + first, count)
+        tile(0, first + count, [(16 + first, count)], False)
+
+    sides = (-1, 1)
+    pair = place(0, 1)
+    take(pair)
+    for side in sides:
+        hop(pair, 2 * side)
+    for side in sides:
+        hop(0, side)
+    take_vector(pair)
+    for side in sides:
+        hop_vector(pair, 2 * side)
+        hop_vector(0, side)
+    for side in sides:
+        take(place(2 * side, 0))
+        hop(place(2 * side, 0), -side)
+    for side in sides:
+        take_vector(place(2 * side, 0))
+        hop_vector(place(2 * side, 0), -side)
+    share(0)
+    compute(0)
+    for side in sides:
+        take(place(2 * side, 1))
+        hop(place(2 * side, 1), -side)
+    for side in sides:
+        hop(pair, side)
+    for side in sides:
+        take_vector(place(2 * side, 1))
+        hop_vector(place(2 * side, 1), -side)
+        hop_vector(pair, side)
+    for side in sides:
+        take(place(side, 0))
+        take_vector(place(side, 0))
+    share(1)
+    for side in sides:
+        take(place(3 * side, 0))
+        hop(place(3 * side, 0), -side, half=(side + 1) // 2)
+    for side in sides:
+        take_vector(place(3 * side, 0))
+    hop_vector(place(-3, 0), 1)
+    compute(1)
+    for side in sides:
+        take(place(3 * side, 1))
+        hop(place(3 * side, 1), -side, half=(side + 1) // 2)
+    for side in sides:
+        take_vector(place(3 * side, 1))
+    hop_vector(place(3, 1), -1)
+    share(3)
+    for side in sides:
+        take(place(side, 1))
+        take_vector(place(side, 1))
+    share(2)
+    compute(2)
+    compute(3)
+    for a in (0, 1):
+        take(place(4, a))
+        take_vector(place(4, a))
+    share(4)
+    compute(4)
+
+    row_far, col_far = far_first(1), far_first(2)
+
+    def to_owner(part, got, s, s_sem, r_sem):
         whole = fold_lanes(acc[SAMP * s : SAMP * s + SAMP, :])
         part[s] = by_group([whole[16 * g : 16 * g + 16] for g in range(4)])
         if s:
-            dz, dxh = offsets(n, j)
-            send(part.at[s], got.at[slot(n, mirror(n, j))], col_peer(dz, dxh), s_sem, r_sem)
-
-    for n, j in far_first:
-        to_owner(part1, got1, n, j, send_sem.at[3], phase_recv.at[0])
+            send(part.at[s], got.at[mirror(s)], col_peer(*SLOTS[s]), s_sem, r_sem)
+
+    for s in col_far + [0]:
+        to_owner(part1, got1, s, send_sem.at[3], phase_recv.at[0])
     wait(got1.at[pl.ds(1, 15)], phase_recv.at[0])
     total = part1[0]
     for s in range(1, 16):
@@ -274,14 +287,12 @@
     vec1[0] = weight
     vec1r[0] = weight
 
-    for n, j in far_first[:-1]:
-        dy, dxl = offsets(n, j)
-        at = slot(n, mirror(n, j))
-        send(vec1.at[0], vec1.at[at], row_peer(dy, dxl, 0), send_sem.at[4], phase_recv.at[1 if n < 4 else 2])
+    for s in row_far:
+        at = mirror(s)
+        send(vec1.at[0], vec1.at[at], row_peer(*SLOTS[s], 0), send_sem.at[4], phase_recv.at[1 if at < 8 else 2])
     send(vec1.at[0], vec1.at[16], sibling, sib_send.at[2], phase_recv.at[3])
-    for n, j in far_first[:-1]:
-        dz, dxh = offsets(n, j)
-        send(vec1r.at[0], vec1r.at[slot(n, mirror(n, j))], col_peer(dz, dxh), send_sem.at[5], phase_recv.at[6])
+    for s in col_far:
+        send(vec1r.at[0], vec1r.at[mirror(s)], col_peer(*SLOTS[s]), send_sem.at[5], phase_recv.at[6])
 
     def second(first, count, fresh, rows):
         columns = pl.ds(first * SAMP, count * SAMP)
@@ -305,8 +316,8 @@
     spread(vec1, 24, 8)
     for chunk in (3, 2, 1, 0):
         second(24, 8, False, pl.ds(256 * chunk, 256))
-        for n, j in far_first[12 - 4 * chunk : 16 - 4 * chunk]:
-            to_owner(part2, got2, n, j, send_sem.at[6], phase_recv.at[7])
+        for s in range(4 * chunk + 3, 4 * chunk - 1, -1):
+            to_owner(part2, got2, s, send_sem.at[6], phase_recv.at[7])
 
     wait(vec1r.at[pl.ds(1, 15)], phase_recv.at[6])
     bend = vec1r[0] * part2[0]
@@ -318,23 +329,20 @@
     both = fold_lanes(jnp.where(first_row, jnp.broadcast_to(bend, (8, 128)), jnp.broadcast_to(squares, (8, 128))))
     dots[0] = both
     two = pl.ds(0, 2)
-    for n, j in far_first:
-        dy, dxl = offsets(n, j)
+    for s in row_far + [0]:
         for dcore in (1, 0):
-            if (n, j, dcore) != (0, 0, 0):
-                at = 16 * dcore + slot(n, mirror(n, j))
-                send(
-                    dots.at[0, two], got_dots.at[at, two], row_peer(dy, dxl, dcore), send_sem.at[7], phase_recv.at[8]
-                )
+            if s or dcore:
+                at = 16 * dcore + mirror(s)
+                to = row_peer(*SLOTS[s], dcore)
+                send(dots.at[0, two], got_dots.at[at, two], to, send_sem.at[7], phase_recv.at[8])
     wait(got_dots.at[pl.ds(1, 31), two], phase_recv.at[8])
     both = both[0:2]
     for s in range(1, 32):
         both = both + got_dots[s, 0:2, :]
     dots[1, 0:2, :] = both
-    for n, j in far_first[:-1]:
-        dz, dxh = offsets(n, j)
-        at = slot(n, mirror(n, j))
-        send(dots.at[1, two], got_dots2.at[at, two], col_peer(dz, dxh), send_sem.at[8], phase_recv.at[9])
+    for s in col_far:
+        to = col_peer(*SLOTS[s])
+        send(dots.at[1, two], got_dots2.at[mirror(s), two], to, send_sem.at[8], phase_recv.at[9])
     wait(got2.at[pl.ds(1, 15)], phase_recv.at[7])
     total = part2[0]
     for s in range(1, 16):
@@ -405,15 +413,15 @@
             dma((4,)),
             dma((9,)),
             dma((3,)),
+            dma((18,)),
+            dma((5,)),
+            dma((18,)),
             dma((16,)),
-            dma((8,)),
-            dma((16,)),
-            dma((16,)),
-            dma((8,)),
+            dma((5,)),
             dma((10,)),
         ],
         compiler_params=pltpu.CompilerParams(
-            collective_id=0, has_side_effects=True, vmem_limit_bytes=48 * 1024 * 1024
+            collective_id=0, has_side_effects=True, vmem_limit_bytes=60 * 1024 * 1024
         ),
     )(states, targets, start_coef, washout.reshape(1, SAMP))
 

time: 69.1 us -> 67.3 us (0.974)
  local copies, waits for them, and re-layouts: 4.13 us -> 1.94 us
    unnamed x10 -> x4, local copies, waits for them, and re-layouts: 4.13 us -> 1.94 us
where the time goes in v3:
time: 67.3 us; the launch traced here: 67.1 us
  Pallas kernels  64.5 us (96%)
  local copies, waits for them, and re-layouts  1.94 us (3%)
    pallas_call x1, Pallas kernels, local(): pl.pallas_call(kernel, out_shape=(out, out), in_specs=[hbm] * 4, out_spec...  64.5 us
    unnamed x4, local copies, waits for them, and re-layouts  1.94 us

profile of v3, /device:TPU:1, one launch (start us, length us, event | category | flops | bytes accessed | tf_op | source)
XLA Modules:
  0.0 67.1 jit_solution(187450543820828434)
XLA Ops:
  0.6 64.5 %shard_map.59 = (f32[32,64]{1,0:T(8,128)}, f32[32,64]{1,0:T(8,128)}) custom-call(bf16[64,512]{1,0:T(8,128)(2,1)} %states_in.1, f32[32,64]{1,0:T(8,128)} %targets_in.1, f32[32,64]{1,0:T(8,128)} %coef_in.1, s32[1,64]{1,0:T(1,128)} %bitcast.1), custom_call_target="tpu_custom_call" | custom-call | tf_op jit(solution)/shard_map/pallas_call | solution.py:387
  65.1 0.0 copy-start
  65.1 1.3 %copy.8 = f32[32,64]{1,0:T(8,128)} copy(f32[32,64]{1,0:T(8,128)} %get-tuple-element.4) | data formatting | bytes 16384
  66.5 0.0 copy-done
  66.5 0.6 copy.9
Async XLA Ops:
  65.1 1.3 %copy-start = (f32[32,64]{1,0:T(8,128)S(1)}, f32[32,64]{1,0:T(8,128)}, u32[]{:S(2)}) copy-start(f32[32,64]{1,0:T(8,128)} %get-tuple-element.5) | copy-start | bytes 24580

commit v4 on v3

--- a/solution.py
+++ b/solution.py
@@ -14,12 +14,13 @@
 OUT = 32
 SLOTS = [
     (0, 0), (0, 1), (-2, 0), (2, 0),
-    (-1, 0), (1, 0), (-2, 1), (2, 1),
-    (-3, 0), (3, 0), (-1, 1), (1, 1),
-    (-3, 1), (3, 1), (4, 0), (4, 1),
+    (-1, 0), (1, 0), (-2, 1), (2, 1), (-3, 0), (3, 0),
+    (-1, 1), (1, 1), (-3, 1), (3, 1),
+    (4, 0), (4, 1),
 ]
 INDEX = {slot: at for at, slot in enumerate(SLOTS)}
-GROUPS = [(0, 4), (4, 4), (8, 4), (12, 2), (14, 2)]
+GROUPS = [(0, 4), (4, 6), (10, 4)]
+SOONER = 14
 EXP_SCALE = math.log2(math.e) * 2.0 / DIM
 
 
@@ -65,7 +66,7 @@
 
 def kernel(
     states_in, targets_in, coef_in, washout_in,
-    coef_out, res_out,
+    both_out,
     states, vectors, washout, col_st, row_st, e_hi, e_lo, w_all, acc, flip,
     vec0, part1, got1, vec1, vec1r, part2, got2, dots, got_dots, got_dots2,
     in_sem, send_sem, sib_send, c_recv, s_recv, r_recv, v_recv, vs_recv, phase_recv,
@@ -115,10 +116,16 @@
         for buf, peer, k, recv in ((row_st, col_peer(d, a), 1, r_recv), (col_st, row_peer(d, a, 0), 0, c_recv)):
             src = buf.at[s, rows] if s else states
             send(src, buf.at[to, rows], peer, send_sem.at[k], recv.at[sem])
+        if half is not None:
+            both = s_recv.at[4 + 2 * half + SLOTS[to][1]]
+            send(col_st.at[s, rows], col_st.at[16 + to, rows], row_peer(d, a, 1), send_sem.at[0], both)
 
     def hop_vector(s, d, a=0):
         to = place(SLOTS[s][0] - d, SLOTS[s][1] + a)
         send(vec0.at[s], vec0.at[to], row_peer(d, a, 0), send_sem.at[2], v_recv.at[to])
+        if SLOTS[to][0] == 4:
+            both = vs_recv.at[1 + SLOTS[to][1]]
+            send(vec0.at[s], vec0.at[16 + to], row_peer(d, a, 1), send_sem.at[2], both)
 
     def take(s):
         for buf, recv in ((row_st, r_recv), (col_st, c_recv)):
@@ -127,15 +134,19 @@
                 wait(buf.at[s, pl.ds(32, 32)], recv.at[16 + SLOTS[s][1]])
             else:
                 wait(buf.at[s], recv.at[s])
+        if SLOTS[s][0] == 4:
+            for half in (0, 1):
+                wait(col_st.at[16 + s, pl.ds(32 * half, 32)], s_recv.at[4 + 2 * half + SLOTS[s][1]])
 
     def take_vector(s):
         wait(vec0.at[s], v_recv.at[s])
+        if SLOTS[s][0] == 4:
+            wait(vec0.at[16 + s], vs_recv.at[1 + SLOTS[s][1]])
 
     def share(g):
         first, count = GROUPS[g]
         own, other = pl.ds(first, count), pl.ds(16 + first, count)
         send(col_st.at[own], col_st.at[other], sibling, sib_send.at[0], s_recv.at[g])
-        send(vec0.at[own], vec0.at[other], sibling, sib_send.at[1], vs_recv.at[g])
 
     hop(0, 0, 1)
     hop(0, 2)
@@ -176,15 +187,17 @@
                 w_all[at : at + 16, 0:128] = jnp.where(keep, hi, 0.0).astype(jnp.bfloat16)
                 w_all[at : at + 16, 128:256] = jnp.where(keep, lo, 0.0).astype(jnp.bfloat16)
 
-    def product(hi, lo, w):
+    def product(rows, ranges):
+        columns = [pl.ds(a * SAMP, k * SAMP) for a, k in ranges]
+        hi, lo = [jnp.concatenate([e[rows, c] for c in columns], axis=1) for e in (e_hi, e_lo)]
+        w = jnp.concatenate([w_all[c, :] for c in columns], axis=0)
         both = jnp.dot(hi, w, preferred_element_type=jnp.float32)
         low = jnp.dot(lo, w[:, 0:128], preferred_element_type=jnp.float32)
         return both[:, 0:128] + both[:, 128:256] + low
 
-    def tile(r_first, r_count, ranges, fresh):
+    def tile(r_first, r_count, ranges):
         left = row_st[r_first : r_first + r_count].reshape(r_count * SAMP, DIM)
         right = jnp.concatenate([col_st[a : a + k].reshape(k * SAMP, DIM) for a, k in ranges], axis=0)
-        w = jnp.concatenate([w_all[a * SAMP : (a + k) * SAMP] for a, k in ranges], axis=0)
         cross = lax.dot_general(left, right, (((1,), (1,)), ((), ())), preferred_element_type=jnp.float32)
         e = jnp.exp2(cross * EXP_SCALE)
         hi = e.astype(jnp.bfloat16)
@@ -196,19 +209,14 @@
             e_hi[rows, columns] = hi[:, at : at + k * SAMP]
             e_lo[rows, columns] = lo[:, at : at + k * SAMP]
             at += k * SAMP
-        add = product(hi, lo, w)
-        acc[rows, :] = add if fresh else acc[rows, :] + add
-
-    def compute(g):
+
+    def grow(g):
         first, count = GROUPS[g]
-        spread(vec0, first, count)
         if first:
-            tile(first, count, [(0, first), (16, first)], True)
-        tile(0, first + count, [(first, count)], first == 0)
+            tile(first, count, [(0, first), (16, first)])
+        tile(0, first + count, [(first, count)])
         wait(col_st.at[pl.ds(16 + first, count)], s_recv.at[g])
-        wait(vec0.at[pl.ds(16 + first, count)], vs_recv.at[g])
-        spread(vec0, 16 + first, count)
-        tile(0, first + count, [(16 + first, count)], False)
+        tile(0, first + count, [(16 + first, count)])
 
     sides = (-1, 1)
     pair = place(0, 1)
@@ -217,56 +225,60 @@
         hop(pair, 2 * side)
     for side in sides:
         hop(0, side)
+    for side in sides:
+        take(place(2 * side, 0))
+        hop(place(2 * side, 0), -side)
+    share(0)
     take_vector(pair)
     for side in sides:
         hop_vector(pair, 2 * side)
         hop_vector(0, side)
     for side in sides:
-        take(place(2 * side, 0))
-        hop(place(2 * side, 0), -side)
-    for side in sides:
         take_vector(place(2 * side, 0))
         hop_vector(place(2 * side, 0), -side)
-    share(0)
-    compute(0)
+    grow(0)
     for side in sides:
         take(place(2 * side, 1))
         hop(place(2 * side, 1), -side)
     for side in sides:
         hop(pair, side)
+    for side in sides:
+        take(place(side, 0))
+    for side in sides:
+        take(place(3 * side, 0))
+        hop(place(3 * side, 0), -side, half=(side + 1) // 2)
+    share(1)
     for side in sides:
         take_vector(place(2 * side, 1))
         hop_vector(place(2 * side, 1), -side)
         hop_vector(pair, side)
-    for side in sides:
-        take(place(side, 0))
         take_vector(place(side, 0))
-    share(1)
-    for side in sides:
-        take(place(3 * side, 0))
-        hop(place(3 * side, 0), -side, half=(side + 1) // 2)
     for side in sides:
         take_vector(place(3 * side, 0))
     hop_vector(place(-3, 0), 1)
-    compute(1)
+    grow(1)
     for side in sides:
         take(place(3 * side, 1))
         hop(place(3 * side, 1), -side, half=(side + 1) // 2)
     for side in sides:
+        take(place(side, 1))
+    share(2)
+    for side in sides:
         take_vector(place(3 * side, 1))
+        take_vector(place(side, 1))
     hop_vector(place(3, 1), -1)
-    share(3)
-    for side in sides:
-        take(place(side, 1))
-        take_vector(place(side, 1))
-    share(2)
-    compute(2)
-    compute(3)
+    sooner, shared = pl.ds(0, SOONER), pl.ds(16, SOONER)
+    send(vec0.at[sooner], vec0.at[shared], sibling, sib_send.at[1], vs_recv.at[0])
+    grow(2)
+    wait(vec0.at[shared], vs_recv.at[0])
+    spread(vec0, 0, SOONER)
+    spread(vec0, 16, SOONER)
+    for first, count in ((0, 256), (256, 256), (512, 256), (768, 128)):
+        rows = pl.ds(first, count)
+        acc[rows, :] = product(rows, [(0, SOONER), (16, SOONER)])
     for a in (0, 1):
         take(place(4, a))
         take_vector(place(4, a))
-    share(4)
-    compute(4)
 
     row_far, col_far = far_first(1), far_first(2)
 
@@ -276,8 +288,19 @@
         if s:
             send(part.at[s], got.at[mirror(s)], col_peer(*SLOTS[s]), s_sem, r_sem)
 
-    for s in col_far + [0]:
-        to_owner(part1, got1, s, send_sem.at[3], phase_recv.at[0])
+    last = [(SOONER, 2), (16 + SOONER, 2)]
+    spread(vec0, SOONER, 2)
+    spread(vec0, 16 + SOONER, 2)
+    tile(SOONER, 2, [(0, SOONER), (16, SOONER)])
+    for first, count in ((14, 2), (10, 4), (6, 4), (4, 2), (0, 4)):
+        rows = pl.ds(first * SAMP, count * SAMP)
+        tile(first, count, last)
+        if first == SOONER:
+            acc[rows, :] = product(rows, [(0, 32)])
+        else:
+            acc[rows, :] += product(rows, last)
+        for s in range(first + count - 1, first - 1, -1):
+            to_owner(part1, got1, s, send_sem.at[3], phase_recv.at[0])
     wait(got1.at[pl.ds(1, 15)], phase_recv.at[0])
     total = part1[0]
     for s in range(1, 16):
@@ -289,33 +312,32 @@
 
     for s in row_far:
         at = mirror(s)
-        send(vec1.at[0], vec1.at[at], row_peer(*SLOTS[s], 0), send_sem.at[4], phase_recv.at[1 if at < 8 else 2])
+        send(vec1.at[0], vec1.at[at], row_peer(*SLOTS[s], 0), send_sem.at[4], phase_recv.at[1 if at < 12 else 2])
     send(vec1.at[0], vec1.at[16], sibling, sib_send.at[2], phase_recv.at[3])
     for s in col_far:
         send(vec1r.at[0], vec1r.at[mirror(s)], col_peer(*SLOTS[s]), send_sem.at[5], phase_recv.at[6])
 
     def second(first, count, fresh, rows):
-        columns = pl.ds(first * SAMP, count * SAMP)
-        add = product(e_hi[rows, columns], e_lo[rows, columns], w_all[columns, :])
+        add = product(rows, [(first, count)])
         acc[rows, :] = add if fresh else acc[rows, :] + add
 
     every = pl.ds(0, 1024)
-    wait(vec1.at[pl.ds(1, 7)], phase_recv.at[1])
-    send(vec1.at[pl.ds(1, 7)], vec1.at[pl.ds(17, 7)], sibling, sib_send.at[2], phase_recv.at[4])
-    spread(vec1, 0, 8)
-    second(0, 8, True, every)
-    wait(vec1.at[pl.ds(8, 8)], phase_recv.at[2])
-    send(vec1.at[pl.ds(8, 8)], vec1.at[pl.ds(24, 8)], sibling, sib_send.at[2], phase_recv.at[5])
-    spread(vec1, 8, 8)
-    second(8, 8, False, every)
+    wait(vec1.at[pl.ds(1, 11)], phase_recv.at[1])
+    send(vec1.at[pl.ds(1, 11)], vec1.at[pl.ds(17, 11)], sibling, sib_send.at[2], phase_recv.at[4])
+    spread(vec1, 0, 12)
+    second(0, 12, True, every)
+    wait(vec1.at[pl.ds(12, 4)], phase_recv.at[2])
+    send(vec1.at[pl.ds(12, 4)], vec1.at[pl.ds(28, 4)], sibling, sib_send.at[2], phase_recv.at[5])
+    spread(vec1, 12, 4)
+    second(12, 4, False, every)
     wait(vec1.at[16], phase_recv.at[3])
-    wait(vec1.at[pl.ds(17, 7)], phase_recv.at[4])
-    spread(vec1, 16, 8)
-    second(16, 8, False, every)
-    wait(vec1.at[pl.ds(24, 8)], phase_recv.at[5])
-    spread(vec1, 24, 8)
+    wait(vec1.at[pl.ds(17, 11)], phase_recv.at[4])
+    spread(vec1, 16, 12)
+    second(16, 12, False, every)
+    wait(vec1.at[pl.ds(28, 4)], phase_recv.at[5])
+    spread(vec1, 28, 4)
     for chunk in (3, 2, 1, 0):
-        second(24, 8, False, pl.ds(256 * chunk, 256))
+        second(28, 4, False, pl.ds(256 * chunk, 256))
         for s in range(4 * chunk + 3, 4 * chunk - 1, -1):
             to_owner(part2, got2, s, send_sem.at[6], phase_recv.at[7])
 
@@ -361,14 +383,14 @@
         b = pltpu.roll(res, (128 + OUT - OUT * g) % 128, axis=1) if g != 1 else res
         flip[16 * g : 16 * g + 16, :] = jnp.where(low, a, b)
     back = flip[...].T
-    coef_out[...] = back[0:OUT, 0:SAMP]
-    res_out[...] = back[OUT : 2 * OUT, 0:SAMP]
-
-    wait(col_st.at[pl.ds(0, 15)], send_sem.at[0])
+    both_out[0] = back[0:OUT, 0:SAMP]
+    both_out[1] = back[OUT : 2 * OUT, 0:SAMP]
+
+    wait(col_st.at[pl.ds(0, 17)], send_sem.at[0])
     wait(row_st.at[pl.ds(0, 15)], send_sem.at[1])
-    wait(vec0.at[pl.ds(0, 15)], send_sem.at[2])
-    wait(col_st.at[pl.ds(0, 16)], sib_send.at[0])
-    wait(vec0.at[pl.ds(0, 16)], sib_send.at[1])
+    wait(vec0.at[pl.ds(0, 17)], send_sem.at[2])
+    wait(col_st.at[pl.ds(0, 14)], sib_send.at[0])
+    wait(vec0.at[pl.ds(0, 14)], sib_send.at[1])
     wait(vec1.at[pl.ds(0, 16)], sib_send.at[2])
     wait(part1.at[pl.ds(0, 15)], send_sem.at[3])
     wait(vec1.at[pl.ds(0, 15)], send_sem.at[4])
@@ -378,17 +400,25 @@
     wait(got_dots2.at[pl.ds(0, 15), two], send_sem.at[8])
 
 
+def store(both, coef_out, res_out, sem):
+    copies = [pltpu.make_async_copy(both.at[k], out, sem.at[k]) for k, out in enumerate((coef_out, res_out))]
+    for copy in copies:
+        copy.start()
+    for copy in copies:
+        copy.wait()
+
+
 def local(states, targets, start_coef, washout):
     f32, bf16 = jnp.float32, jnp.bfloat16
     vmem = pl.BlockSpec(memory_space=pltpu.VMEM)
     hbm = pl.BlockSpec(memory_space=pltpu.HBM)
-    out = jax.ShapeDtypeStruct((OUT, SAMP), f32)
     dma = pltpu.SemaphoreType.DMA
-    return pl.pallas_call(
+    inputs = (states, targets, start_coef, washout.reshape(1, SAMP))
+    both = pl.pallas_call(
         kernel,
-        out_shape=(out, out),
+        out_shape=pltpu.VMEM((2, OUT, SAMP), f32),
         in_specs=[hbm] * 4,
-        out_specs=(vmem, vmem),
+        out_specs=vmem,
         scratch_shapes=[
             pltpu.VMEM((SAMP, DIM), bf16),
             pltpu.VMEM((2, OUT, SAMP), f32),
@@ -414,16 +444,24 @@
             dma((9,)),
             dma((3,)),
             dma((18,)),
-            dma((5,)),
+            dma((8,)),
             dma((18,)),
             dma((16,)),
-            dma((5,)),
+            dma((6,)),
             dma((10,)),
         ],
         compiler_params=pltpu.CompilerParams(
-            collective_id=0, has_side_effects=True, vmem_limit_bytes=60 * 1024 * 1024
+            collective_id=0, has_side_effects=True, vmem_limit_bytes=48 * 1024 * 1024
         ),
-    )(states, targets, start_coef, washout.reshape(1, SAMP))
+    )(*[pltpu.with_memory_space_constraint(x, pltpu.HBM) for x in inputs])
+    out = jax.ShapeDtypeStruct((OUT, SAMP), f32)
+    return pl.pallas_call(
+        store,
+        out_shape=(out, out),
+        in_specs=[vmem],
+        out_specs=(hbm, hbm),
+        scratch_shapes=[dma((2,))],
+    )(both)
 
 
 def solution(mesh):

time: 67.3 us -> 66.1 us (0.982)
  local copies, waits for them, and re-layouts: 1.94 us -> 0.61 us
    unnamed x4 -> x2, local copies, waits for them, and re-layouts: 1.94 us -> 0.61 us
    pallas_call x1 -> x2, Pallas kernels: 64.5 us -> 64.6 us  [the longest x1 63.2 us: local(): pl.pallas_call(kernel, out_shape=pltpu.VMEM((2, OUT, SAMP), f32), in_spec...]
where the time goes in v4:
time: 66.1 us; the launch traced here: 65.9 us
  Pallas kernels  64.6 us (98%)
    pallas_call x1, Pallas kernels, local(): pl.pallas_call(kernel, out_shape=pltpu.VMEM((2, OUT, SAMP), f32), in_spec...  63.2 us
    pallas_call x1, Pallas kernels, local(): pl.pallas_call(store, out_shape=(out, out), in_specs=[vmem], out_specs=(h...  1.38 us

profile of v4, /device:TPU:1, one launch (start us, length us, event | category | flops | bytes accessed | tf_op | source)
XLA Modules:
  0.0 65.9 jit_solution(7558311317195976108)
XLA Ops:
  0.6 63.2 %shard_map.59.both = f32[2,32,64]{2,1,0:T(8,128)S(1)} custom-call(bf16[64,512]{1,0:T(8,128)(2,1)} %states_in.1, f32[32,64]{1,0:T(8,128)} %targets_in.1, f32[32,64]{1,0:T(8,128)} %coef_in.1, s32[1,64]{1,0:T(1,128)} %bitcast.1), custom_call_target="tpu_custom_call" | custom-call | tf_op jit(solution)/shard_map/pallas_call | solution.py:417
  63.9 0.0 copy-start
  63.9 0.6 copy-done
  64.5 1.4 %shard_map.60 = (f32[32,64]{1,0:T(8,128)}, f32[32,64]{1,0:T(8,128)}) custom-call(f32[2,32,64]{2,1,0:T(8,128)} %copy-done), custom_call_target="tpu_custom_call" | custom-call | tf_op jit(solution)/shard_map/pallas_call | solution.py:458
Async XLA Ops:
  63.9 0.6 copy-start

commit v5 on v4

--- a/solution.py
+++ b/solution.py
@@ -21,6 +21,8 @@
 INDEX = {slot: at for at, slot in enumerate(SLOTS)}
 GROUPS = [(0, 4), (4, 6), (10, 4)]
 SOONER = 14
+ROW_SLOT = 4 * SAMP
+COL_SLOT = ROW_SLOT + 32
 EXP_SCALE = math.log2(math.e) * 2.0 / DIM
 
 
@@ -68,8 +70,8 @@
     states_in, targets_in, coef_in, washout_in,
     both_out,
     states, vectors, washout, col_st, row_st, e_hi, e_lo, w_all, acc, flip,
-    vec0, part1, got1, vec1, vec1r, part2, got2, dots, got_dots, got_dots2,
-    in_sem, send_sem, sib_send, c_recv, s_recv, r_recv, v_recv, vs_recv, phase_recv,
+    part1, got1, vec1, vec1r, part2, got2, dots, got_dots, got_dots2,
+    in_sem, send_sem, sib_send, c_recv, s_recv, r_recv, phase_recv,
 ):
     row, col = lax.axis_index("row"), lax.axis_index("col")
     core, xl, y = row % 2, (row // 2) % 2, row // 4
@@ -99,7 +101,6 @@
     for fetch in fetches:
         fetch.start()
     fetches[0].wait()
-    pl.semaphore_wait(barrier, len(near))
 
     def send(src, dst, to, s_sem, r_sem):
         pltpu.make_async_remote_copy(
@@ -109,51 +110,48 @@
     def wait(ref, sem):
         pltpu.make_async_copy(ref, ref, sem).wait()
 
-    def hop(s, d, a=0, half=None):
+    def send_col(s, d, a=0, half=None):
         to = place(SLOTS[s][0] - d, SLOTS[s][1] + a)
-        rows = pl.ds(0, SAMP) if half is None else pl.ds(half * 32, 32)
-        sem = to if half is None or half == 0 else 16 + SLOTS[to][1]
-        for buf, peer, k, recv in ((row_st, col_peer(d, a), 1, r_recv), (col_st, row_peer(d, a, 0), 0, c_recv)):
-            src = buf.at[s, rows] if s else states
-            send(src, buf.at[to, rows], peer, send_sem.at[k], recv.at[sem])
+        rows = pl.ds(0, COL_SLOT) if half is None else pl.ds(half * (COL_SLOT // 2), COL_SLOT // 2)
+        sem = 16 + SLOTS[to][1] if half else to
+        src = col_st.at[s, rows]
+        send(src, col_st.at[to, rows], row_peer(d, a, 0), send_sem.at[0], c_recv.at[sem])
         if half is not None:
             both = s_recv.at[4 + 2 * half + SLOTS[to][1]]
-            send(col_st.at[s, rows], col_st.at[16 + to, rows], row_peer(d, a, 1), send_sem.at[0], both)
-
-    def hop_vector(s, d, a=0):
+            send(src, col_st.at[16 + to, rows], row_peer(d, a, 1), send_sem.at[0], both)
+
+    def send_row(s, d, a=0, half=None):
         to = place(SLOTS[s][0] - d, SLOTS[s][1] + a)
-        send(vec0.at[s], vec0.at[to], row_peer(d, a, 0), send_sem.at[2], v_recv.at[to])
-        if SLOTS[to][0] == 4:
-            both = vs_recv.at[1 + SLOTS[to][1]]
-            send(vec0.at[s], vec0.at[16 + to], row_peer(d, a, 1), send_sem.at[2], both)
-
-    def take(s):
-        for buf, recv in ((row_st, r_recv), (col_st, c_recv)):
-            if SLOTS[s][0] == 4:
-                wait(buf.at[s, pl.ds(0, 32)], recv.at[s])
-                wait(buf.at[s, pl.ds(32, 32)], recv.at[16 + SLOTS[s][1]])
-            else:
-                wait(buf.at[s], recv.at[s])
+        rows = pl.ds(0, ROW_SLOT) if half is None else pl.ds(half * (ROW_SLOT // 2), ROW_SLOT // 2)
+        sem = 16 + SLOTS[to][1] if half else to
+        send(row_st.at[s, rows], row_st.at[to, rows], col_peer(d, a), send_sem.at[1], r_recv.at[sem])
+
+    def take_col(s):
         if SLOTS[s][0] == 4:
             for half in (0, 1):
-                wait(col_st.at[16 + s, pl.ds(32 * half, 32)], s_recv.at[4 + 2 * half + SLOTS[s][1]])
-
-    def take_vector(s):
-        wait(vec0.at[s], v_recv.at[s])
+                rows = pl.ds(half * (COL_SLOT // 2), COL_SLOT // 2)
+                wait(col_st.at[s, rows], c_recv.at[16 + SLOTS[s][1] if half else s])
+                wait(col_st.at[16 + s, rows], s_recv.at[4 + 2 * half + SLOTS[s][1]])
+        else:
+            wait(col_st.at[s], c_recv.at[s])
+
+    def take_row(s):
         if SLOTS[s][0] == 4:
-            wait(vec0.at[16 + s], vs_recv.at[1 + SLOTS[s][1]])
+            for half in (0, 1):
+                rows = pl.ds(half * (ROW_SLOT // 2), ROW_SLOT // 2)
+                wait(row_st.at[s, rows], r_recv.at[16 + SLOTS[s][1] if half else s])
+        else:
+            wait(row_st.at[s], r_recv.at[s])
 
     def share(g):
         first, count = GROUPS[g]
         own, other = pl.ds(first, count), pl.ds(16 + first, count)
         send(col_st.at[own], col_st.at[other], sibling, sib_send.at[0], s_recv.at[g])
 
-    hop(0, 0, 1)
-    hop(0, 2)
-    hop(0, -2)
-    col_st[0] = states[...]
-    row_st[0] = states[...]
-
+    for k in range(4):
+        piece = states[:, 128 * k : 128 * k + 128]
+        col_st[0, SAMP * k : SAMP * k + SAMP, :] = piece
+        row_st[0, SAMP * k : SAMP * k + SAMP, :] = piece
     own_f = states[...].astype(jnp.float32)
     norm = jnp.sum(own_f * own_f, axis=1, keepdims=True)
     damp_col = jnp.broadcast_to(jnp.exp(norm * (-1.0 / DIM)), (SAMP, 128))
@@ -168,24 +166,36 @@
     target = pack(turned, 0) * mask
     start = pack(turned, 1)
     scale = mask * damp
-    vec0[0] = scale * start
-
-    hop_vector(0, 0, 1)
-    hop_vector(0, 2)
-    hop_vector(0, -2)
+    weight = scale * start
+    high = weight.astype(jnp.bfloat16)
+    col_st[0, ROW_SLOT : ROW_SLOT + 16, :] = high
+    col_st[0, ROW_SLOT + 16 : COL_SLOT, :] = (weight - high.astype(jnp.float32)).astype(jnp.bfloat16)
+    pl.semaphore_wait(barrier, len(near))
+
+    for way in (send_col, send_row):
+        way(0, 0, 1)
+        way(0, 2)
+        way(0, -2)
 
     group = lane_group()
+
+    def lay(s, hi, lo):
+        for g in range(4):
+            keep = group == g
+            at = SAMP * s + 16 * g
+            w_all[at : at + 16, 0:128] = jnp.where(keep, hi, 0.0).astype(jnp.bfloat16)
+            w_all[at : at + 16, 128:256] = jnp.where(keep, lo, 0.0).astype(jnp.bfloat16)
+
+    def spread_sent(first, count):
+        for s in range(first, first + count):
+            hi = col_st[s, ROW_SLOT : ROW_SLOT + 16, :]
+            lo = col_st[s, ROW_SLOT + 16 : COL_SLOT, :]
+            lay(s, hi.astype(jnp.float32), lo.astype(jnp.float32))
 
     def spread(vec, first, count):
         for s in range(first, first + count):
-            v = vec[s]
-            hi = v.astype(jnp.bfloat16).astype(jnp.float32)
-            lo = v - hi
-            for g in range(4):
-                keep = group == g
-                at = SAMP * s + 16 * g
-                w_all[at : at + 16, 0:128] = jnp.where(keep, hi, 0.0).astype(jnp.bfloat16)
-                w_all[at : at + 16, 128:256] = jnp.where(keep, lo, 0.0).astype(jnp.bfloat16)
+            hi = vec[s].astype(jnp.bfloat16).astype(jnp.float32)
+            lay(s, hi, vec[s] - hi)
 
     def product(rows, ranges):
         columns = [pl.ds(a * SAMP, k * SAMP) for a, k in ranges]
@@ -195,9 +205,18 @@
         low = jnp.dot(lo, w[:, 0:128], preferred_element_type=jnp.float32)
         return both[:, 0:128] + both[:, 128:256] + low
 
+    def slots_of(buf, first, count):
+        return jnp.concatenate(
+            [
+                jnp.concatenate([buf[s, SAMP * k : SAMP * k + SAMP, :] for k in range(4)], axis=1)
+                for s in range(first, first + count)
+            ],
+            axis=0,
+        )
+
     def tile(r_first, r_count, ranges):
-        left = row_st[r_first : r_first + r_count].reshape(r_count * SAMP, DIM)
-        right = jnp.concatenate([col_st[a : a + k].reshape(k * SAMP, DIM) for a, k in ranges], axis=0)
+        left = slots_of(row_st, r_first, r_count)
+        right = jnp.concatenate([slots_of(col_st, a, k) for a, k in ranges], axis=0)
         cross = lax.dot_general(left, right, (((1,), (1,)), ((), ())), preferred_element_type=jnp.float32)
         e = jnp.exp2(cross * EXP_SCALE)
         hi = e.astype(jnp.bfloat16)
@@ -210,75 +229,72 @@
             e_lo[rows, columns] = lo[:, at : at + k * SAMP]
             at += k * SAMP
 
-    def grow(g):
+    def grow_own(g):
         first, count = GROUPS[g]
         if first:
             tile(first, count, [(0, first), (16, first)])
         tile(0, first + count, [(first, count)])
+
+    def grow_other(g):
+        first, count = GROUPS[g]
         wait(col_st.at[pl.ds(16 + first, count)], s_recv.at[g])
         tile(0, first + count, [(16 + first, count)])
 
     sides = (-1, 1)
     pair = place(0, 1)
-    take(pair)
-    for side in sides:
-        hop(pair, 2 * side)
-    for side in sides:
-        hop(0, side)
-    for side in sides:
-        take(place(2 * side, 0))
-        hop(place(2 * side, 0), -side)
+    chains = ((take_col, send_col), (take_row, send_row))
+    for take, pass_on in chains:
+        take(pair)
+        for side in sides:
+            pass_on(pair, 2 * side)
+        for side in sides:
+            pass_on(0, side)
+    for take, pass_on in chains:
+        for side in sides:
+            take(place(2 * side, 0))
+            pass_on(place(2 * side, 0), -side)
     share(0)
-    take_vector(pair)
-    for side in sides:
-        hop_vector(pair, 2 * side)
-        hop_vector(0, side)
-    for side in sides:
-        take_vector(place(2 * side, 0))
-        hop_vector(place(2 * side, 0), -side)
-    grow(0)
-    for side in sides:
-        take(place(2 * side, 1))
-        hop(place(2 * side, 1), -side)
-    for side in sides:
-        hop(pair, side)
-    for side in sides:
-        take(place(side, 0))
-    for side in sides:
-        take(place(3 * side, 0))
-        hop(place(3 * side, 0), -side, half=(side + 1) // 2)
+    grow_own(0)
+    grow_other(0)
+    for take, pass_on in chains:
+        for side in sides:
+            take(place(2 * side, 1))
+            pass_on(place(2 * side, 1), -side)
+        for side in sides:
+            pass_on(pair, side)
+    for take, pass_on in chains:
+        for side in sides:
+            take(place(side, 0))
+        for side in sides:
+            take(place(3 * side, 0))
+            pass_on(place(3 * side, 0), -side, half=(side + 1) // 2)
     share(1)
-    for side in sides:
-        take_vector(place(2 * side, 1))
-        hop_vector(place(2 * side, 1), -side)
-        hop_vector(pair, side)
-        take_vector(place(side, 0))
-    for side in sides:
-        take_vector(place(3 * side, 0))
-    hop_vector(place(-3, 0), 1)
-    grow(1)
-    for side in sides:
-        take(place(3 * side, 1))
-        hop(place(3 * side, 1), -side, half=(side + 1) // 2)
-    for side in sides:
-        take(place(side, 1))
+    grow_own(1)
+    grow_other(1)
+    for take, pass_on in chains:
+        for side in sides:
+            take(place(3 * side, 1))
+            pass_on(place(3 * side, 1), -side, half=(side + 1) // 2)
+        for side in sides:
+            take(place(side, 1))
     share(2)
-    for side in sides:
-        take_vector(place(3 * side, 1))
-        take_vector(place(side, 1))
-    hop_vector(place(3, 1), -1)
-    sooner, shared = pl.ds(0, SOONER), pl.ds(16, SOONER)
-    send(vec0.at[sooner], vec0.at[shared], sibling, sib_send.at[1], vs_recv.at[0])
-    grow(2)
-    wait(vec0.at[shared], vs_recv.at[0])
-    spread(vec0, 0, SOONER)
-    spread(vec0, 16, SOONER)
-    for first, count in ((0, 256), (256, 256), (512, 256), (768, 128)):
+    before = GROUPS[2][0]
+    grow_own(2)
+    for first in (0, 16):
+        spread_sent(first, before)
+    for first, count in ((0, 256), (256, 256), (512, 128)):
         rows = pl.ds(first, count)
-        acc[rows, :] = product(rows, [(0, SOONER), (16, SOONER)])
+        acc[rows, :] = product(rows, [(0, before), (16, before)])
+    grow_other(2)
+    for first in (0, 16):
+        spread_sent(first + before, SOONER - before)
+    for first, count in ((0, 256), (256, 256), (512, 128)):
+        rows = pl.ds(first, count)
+        acc[rows, :] += product(rows, [(before, SOONER - before), (16 + before, SOONER - before)])
+    rows = pl.ds(before * SAMP, (SOONER - before) * SAMP)
+    acc[rows, :] = product(rows, [(0, SOONER), (16, SOONER)])
     for a in (0, 1):
-        take(place(4, a))
-        take_vector(place(4, a))
+        take_col(place(4, a))
 
     row_far, col_far = far_first(1), far_first(2)
 
@@ -289,12 +305,14 @@
             send(part.at[s], got.at[mirror(s)], col_peer(*SLOTS[s]), s_sem, r_sem)
 
     last = [(SOONER, 2), (16 + SOONER, 2)]
-    spread(vec0, SOONER, 2)
-    spread(vec0, 16 + SOONER, 2)
-    tile(SOONER, 2, [(0, SOONER), (16, SOONER)])
+    spread_sent(SOONER, 2)
+    spread_sent(16 + SOONER, 2)
+    tile(0, SOONER, last)
+    for a in (0, 1):
+        take_row(place(4, a))
+    tile(SOONER, 2, [(0, 32)])
     for first, count in ((14, 2), (10, 4), (6, 4), (4, 2), (0, 4)):
         rows = pl.ds(first * SAMP, count * SAMP)
-        tile(first, count, last)
         if first == SOONER:
             acc[rows, :] = product(rows, [(0, 32)])
         else:
@@ -388,9 +406,7 @@
 
     wait(col_st.at[pl.ds(0, 17)], send_sem.at[0])
     wait(row_st.at[pl.ds(0, 15)], send_sem.at[1])
-    wait(vec0.at[pl.ds(0, 17)], send_sem.at[2])
     wait(col_st.at[pl.ds(0, 14)], sib_send.at[0])
-    wait(vec0.at[pl.ds(0, 14)], sib_send.at[1])
     wait(vec1.at[pl.ds(0, 16)], sib_send.at[2])
     wait(part1.at[pl.ds(0, 15)], send_sem.at[3])
     wait(vec1.at[pl.ds(0, 15)], send_sem.at[4])
@@ -423,14 +439,13 @@
             pltpu.VMEM((SAMP, DIM), bf16),
             pltpu.VMEM((2, OUT, SAMP), f32),
             pltpu.VMEM((1, SAMP), jnp.int32),
-            pltpu.VMEM((32, SAMP, DIM), bf16),
-            pltpu.VMEM((16, SAMP, DIM), bf16),
+            pltpu.VMEM((32, COL_SLOT, 128), bf16),
+            pltpu.VMEM((16, ROW_SLOT, 128), bf16),
             pltpu.VMEM((1024, 2048), bf16),
             pltpu.VMEM((1024, 2048), bf16),
             pltpu.VMEM((2048, 256), bf16),
             pltpu.VMEM((1024, 128), f32),
             pltpu.VMEM((128, 128), f32),
-            pltpu.VMEM((32, 16, 128), f32),
             pltpu.VMEM((16, 16, 128), f32),
             pltpu.VMEM((16, 16, 128), f32),
             pltpu.VMEM((32, 16, 128), f32),
@@ -446,8 +461,6 @@
             dma((18,)),
             dma((8,)),
             dma((18,)),
-            dma((16,)),
-            dma((6,)),
             dma((10,)),
         ],
         compiler_params=pltpu.CompilerParams(
@@ -461,6 +474,7 @@
         in_specs=[vmem],
         out_specs=(hbm, hbm),
         scratch_shapes=[dma((2,))],
+        compiler_params=pltpu.CompilerParams(vmem_limit_bytes=2 * 1024 * 1024),
     )(both)
 
 

time: 66.1 us -> 64.1 us (0.970)
  Pallas kernels: 64.6 us -> 63.3 us
    pallas_call x1, Pallas kernels: 1.38 us -> 0.63 us  [local(): pl.pallas_call(store, out_shape=(out, out), in_specs=[vmem], out_specs=(h...]
where the time goes in v5:
time: 64.1 us; the launch traced here: 63.9 us
  Pallas kernels  63.3 us (99%)
    pallas_call x1, Pallas kernels, local(): pl.pallas_call(kernel, out_shape=pltpu.VMEM((2, OUT, SAMP), f32), in_spec...  62.6 us

profile of v5, /device:TPU:1, one launch (start us, length us, event | category | flops | bytes accessed | tf_op | source)
XLA Modules:
  0.0 63.9 jit_solution(6758588297463515013)
XLA Ops:
  0.6 62.6 %shard_map.59.both = f32[2,32,64]{2,1,0:T(8,128)S(1)} custom-call(bf16[64,512]{1,0:T(8,128)(2,1)} %states_in.1, f32[32,64]{1,0:T(8,128)} %targets_in.1, f32[32,64]{1,0:T(8,128)} %coef_in.1, s32[1,64]{1,0:T(1,128)} %bitcast.1), custom_call_target="tpu_custom_call" | custom-call | tf_op jit(solution)/shard_map/pallas_call | solution.py:433
  63.3 0.6 shard_map.60

commit v6 on v5

--- a/solution.py
+++ b/solution.py
@@ -32,6 +32,12 @@
 
 def mirror(s):
     return place(-SLOTS[s][0], SLOTS[s][1])
+
+
+CHIPS = sorted(
+    [(dx, dy, dz) for dx in range(4) for dy in range(RING) for dz in range(RING) if dx or dy or dz],
+    key=lambda d: -min(d[0], 4 - d[0]) - min(d[1], RING - d[1]) - min(d[2], RING - d[2]),
+)
 
 
 def far_first(pair_hops):
@@ -365,34 +371,34 @@
         bend = bend + vec1r[s] * part2[s]
     bend = jnp.sum(bend, axis=0, keepdims=True)
     squares = jnp.sum(r0 * r0, axis=0, keepdims=True)
-    first_row = lax.broadcasted_iota(jnp.int32, (8, 128), 0) == 0
-    both = fold_lanes(jnp.where(first_row, jnp.broadcast_to(bend, (8, 128)), jnp.broadcast_to(squares, (8, 128))))
-    dots[0] = both
-    two = pl.ds(0, 2)
-    for s in row_far + [0]:
-        for dcore in (1, 0):
-            if s or dcore:
-                at = 16 * dcore + mirror(s)
-                to = row_peer(*SLOTS[s], dcore)
-                send(dots.at[0, two], got_dots.at[at, two], to, send_sem.at[7], phase_recv.at[8])
-    wait(got_dots.at[pl.ds(1, 31), two], phase_recv.at[8])
-    both = both[0:2]
-    for s in range(1, 32):
-        both = both + got_dots[s, 0:2, :]
-    dots[1, 0:2, :] = both
-    for s in col_far:
-        to = col_peer(*SLOTS[s])
-        send(dots.at[1, two], got_dots2.at[mirror(s), two], to, send_sem.at[8], phase_recv.at[9])
+    leading = lax.broadcasted_iota(jnp.int32, (1, 128), 1) < OUT
+    line = jnp.where(leading, fold_lanes(bend), fold_lanes(squares))
+    dots[0:1, :] = line
+    got_dots[0:1, :] = line
+    x = xh * 2 + xl
+    at_x = [(x + d) % 4 for d in range(4)]
+    rows_x = [(v % 2) * 2 + core for v in at_x]
+    cols_x = [v // 2 for v in at_x]
+    rows_y = [(y + d) % RING * 4 for d in range(RING)]
+    cols_z = [(z + d) % RING * 2 for d in range(RING)]
+    for dx, dy, dz in CHIPS:
+        back = (-dx % 4 * RING + -dy % RING) * RING + -dz % RING
+        to = (rows_y[dy] + rows_x[dx], cols_z[dz] + cols_x[dx])
+        send(dots.at[pl.ds(0, 1)], got_dots.at[pl.ds(back, 1)], to, send_sem.at[7], phase_recv.at[8])
     wait(got2.at[pl.ds(1, 15)], phase_recv.at[7])
     total = part2[0]
     for s in range(1, 16):
         total = total + got2[s]
     q = scale * total + r0
-    wait(got_dots2.at[pl.ds(1, 15), two], phase_recv.at[9])
-    for s in range(1, 16):
-        both = both + got_dots2[s, 0:2, :]
-    squares = both[1:2]
-    alpha = squares / (both[0:1] + squares)
+    wait(got_dots.at[pl.ds(1, 255)], phase_recv.at[8])
+    line = jnp.sum(jnp.sum(got_dots[...].reshape(32, 8, 128), axis=0), axis=0, keepdims=True)
+    dots[1:2, :] = line
+    send(dots.at[pl.ds(1, 1)], got_dots2.at[pl.ds(0, 1)], sibling, send_sem.at[8], phase_recv.at[9])
+    wait(got_dots2.at[pl.ds(0, 1)], phase_recv.at[9])
+    line = line + got_dots2[0:1, :]
+    bend = fold_lanes(jnp.where(leading, line, 0.0))
+    squares = jnp.where(leading, pltpu.roll(line, 128 - OUT, axis=1), line)
+    alpha = squares / (bend + squares)
     coef = start + alpha * r0
     res = r0 - alpha * q
     low = lax.broadcasted_iota(jnp.int32, (16, 128), 1) < OUT
@@ -412,8 +418,8 @@
     wait(vec1.at[pl.ds(0, 15)], send_sem.at[4])
     wait(vec1r.at[pl.ds(0, 15)], send_sem.at[5])
     wait(part2.at[pl.ds(0, 15)], send_sem.at[6])
-    wait(got_dots.at[pl.ds(0, 31), two], send_sem.at[7])
-    wait(got_dots2.at[pl.ds(0, 15), two], send_sem.at[8])
+    wait(got_dots.at[pl.ds(0, 255)], send_sem.at[7])
+    wait(got_dots2.at[pl.ds(0, 1)], send_sem.at[8])
 
 
 def store(both, coef_out, res_out, sem):
@@ -452,9 +458,9 @@
             pltpu.VMEM((16, 16, 128), f32),
             pltpu.VMEM((16, 16, 128), f32),
             pltpu.VMEM((16, 16, 128), f32),
-            pltpu.VMEM((2, 8, 128), f32),
-            pltpu.VMEM((32, 8, 128), f32),
-            pltpu.VMEM((16, 8, 128), f32),
+            pltpu.VMEM((8, 128), f32),
+            pltpu.VMEM((256, 128), f32),
+            pltpu.VMEM((8, 128), f32),
             dma((4,)),
             dma((9,)),
             dma((3,)),

time: 64.1 us -> 63.9 us (level)
  no operation moved by 1% of the time
where the time goes in v6:
time: 63.9 us; the launch traced here: 63.7 us
  Pallas kernels  63.1 us (99%)
  between operations  0.64 us (1%)
    pallas_call x1, Pallas kernels, local(): pl.pallas_call(kernel, out_shape=pltpu.VMEM((2, OUT, SAMP), f32), in_spec...  62.4 us

profile of v6, /device:TPU:1, one launch (start us, length us, event | category | flops | bytes accessed | tf_op | source)
XLA Modules:
  0.0 63.7 jit_solution(9690722787745889144)
XLA Ops:
  0.6 62.4 %shard_map.59.both = f32[2,32,64]{2,1,0:T(8,128)S(1)} custom-call(bf16[64,512]{1,0:T(8,128)(2,1)} %states_in.1, f32[32,64]{1,0:T(8,128)} %targets_in.1, f32[32,64]{1,0:T(8,128)} %coef_in.1, s32[1,64]{1,0:T(1,128)} %bitcast.1), custom_call_target="tpu_custom_call" | custom-call | tf_op jit(solution)/shard_map/pallas_call | solution.py:439
  63.1 0.6 shard_map.60

commit v7 on v6

--- a/solution.py
+++ b/solution.py
@@ -106,7 +106,6 @@
     ]
     for fetch in fetches:
         fetch.start()
-    fetches[0].wait()
 
     def send(src, dst, to, s_sem, r_sem):
         pltpu.make_async_remote_copy(
@@ -153,6 +152,17 @@
         first, count = GROUPS[g]
         own, other = pl.ds(first, count), pl.ds(16 + first, count)
         send(col_st.at[own], col_st.at[other], sibling, sib_send.at[0], s_recv.at[g])
+
+    pl.semaphore_wait(barrier, len(near))
+    first_ways = [(0, 1), (2, 0), (-2, 0)]
+    for d, a in first_ways:
+        to = place(-d, a)
+        for k in range(4):
+            piece = states_in.at[:, pl.ds(128 * k, 128)]
+            rows = pl.ds(SAMP * k, SAMP)
+            send(piece, col_st.at[to, rows], row_peer(d, a, 0), send_sem.at[0], c_recv.at[to])
+            send(piece, row_st.at[to, rows], col_peer(d, a), send_sem.at[1], r_recv.at[to])
+    fetches[0].wait()
 
     for k in range(4):
         piece = states[:, 128 * k : 128 * k + 128]
@@ -176,12 +186,10 @@
     high = weight.astype(jnp.bfloat16)
     col_st[0, ROW_SLOT : ROW_SLOT + 16, :] = high
     col_st[0, ROW_SLOT + 16 : COL_SLOT, :] = (weight - high.astype(jnp.float32)).astype(jnp.bfloat16)
-    pl.semaphore_wait(barrier, len(near))
-
-    for way in (send_col, send_row):
-        way(0, 0, 1)
-        way(0, 2)
-        way(0, -2)
+    for d, a in first_ways:
+        rows = pl.ds(ROW_SLOT, 32)
+        to = place(-d, a)
+        send(col_st.at[0, rows], col_st.at[to, rows], row_peer(d, a, 0), send_sem.at[0], c_recv.at[to])
 
     group = lane_group()
 
@@ -313,7 +321,6 @@
     last = [(SOONER, 2), (16 + SOONER, 2)]
     spread_sent(SOONER, 2)
     spread_sent(16 + SOONER, 2)
-    tile(0, SOONER, last)
     for a in (0, 1):
         take_row(place(4, a))
     tile(SOONER, 2, [(0, 32)])
@@ -322,6 +329,7 @@
         if first == SOONER:
             acc[rows, :] = product(rows, [(0, 32)])
         else:
+            tile(first, count, last)
             acc[rows, :] += product(rows, last)
         for s in range(first + count - 1, first - 1, -1):
             to_owner(part1, got1, s, send_sem.at[3], phase_recv.at[0])

time: 63.9 us -> 63.5 us (level)
  no operation moved by 1% of the time
where the time goes in v7:
time: 63.5 us; the launch traced here: 63.4 us
  Pallas kernels  62.8 us (99%)
  between operations  0.64 us (1%)
    pallas_call x1, Pallas kernels, local(): pl.pallas_call(kernel, out_shape=pltpu.VMEM((2, OUT, SAMP), f32), in_spec...  62.1 us

profile of v7, /device:TPU:1, one launch (start us, length us, event | category | flops | bytes accessed | tf_op | source)
XLA Modules:
  0.0 63.4 jit_solution(13560974150548558317)
XLA Ops:
  0.6 62.1 %shard_map.59.both = f32[2,32,64]{2,1,0:T(8,128)S(1)} custom-call(bf16[64,512]{1,0:T(8,128)(2,1)} %states_in.1, f32[32,64]{1,0:T(8,128)} %targets_in.1, f32[32,64]{1,0:T(8,128)} %coef_in.1, s32[1,64]{1,0:T(1,128)} %bitcast.1), custom_call_target="tpu_custom_call" | custom-call | tf_op jit(solution)/shard_map/pallas_call | solution.py:447
  62.8 0.6 shard_map.60

commit v8 on v7

--- a/solution.py
+++ b/solution.py
@@ -393,15 +393,15 @@
         back = (-dx % 4 * RING + -dy % RING) * RING + -dz % RING
         to = (rows_y[dy] + rows_x[dx], cols_z[dz] + cols_x[dx])
         send(dots.at[pl.ds(0, 1)], got_dots.at[pl.ds(back, 1)], to, send_sem.at[7], phase_recv.at[8])
+    wait(got_dots.at[pl.ds(1, 255)], phase_recv.at[8])
+    line = jnp.sum(jnp.sum(got_dots[...].reshape(32, 8, 128), axis=0), axis=0, keepdims=True)
+    dots[1:2, :] = line
+    send(dots.at[pl.ds(1, 1)], got_dots2.at[pl.ds(0, 1)], sibling, send_sem.at[8], phase_recv.at[9])
     wait(got2.at[pl.ds(1, 15)], phase_recv.at[7])
     total = part2[0]
     for s in range(1, 16):
         total = total + got2[s]
     q = scale * total + r0
-    wait(got_dots.at[pl.ds(1, 255)], phase_recv.at[8])
-    line = jnp.sum(jnp.sum(got_dots[...].reshape(32, 8, 128), axis=0), axis=0, keepdims=True)
-    dots[1:2, :] = line
-    send(dots.at[pl.ds(1, 1)], got_dots2.at[pl.ds(0, 1)], sibling, send_sem.at[8], phase_recv.at[9])
     wait(got_dots2.at[pl.ds(0, 1)], phase_recv.at[9])
     line = line + got_dots2[0:1, :]
     bend = fold_lanes(jnp.where(leading, line, 0.0))

time: 63.5 us -> 63.5 us (level)
  no operation moved by 1% of the time
where the time goes in v8:
time: 63.5 us; the launch traced here: 63.4 us
  Pallas kernels  62.8 us (99%)
  between operations  0.64 us (1%)
    pallas_call x1, Pallas kernels, local(): pl.pallas_call(kernel, out_shape=pltpu.VMEM((2, OUT, SAMP), f32), in_spec...  62.1 us

profile of v8, /device:TPU:1, one launch (start us, length us, event | category | flops | bytes accessed | tf_op | source)
XLA Modules:
  0.0 63.4 jit_solution(15836417085652699112)
XLA Ops:
  0.6 62.1 %shard_map.59.both = f32[2,32,64]{2,1,0:T(8,128)S(1)} custom-call(bf16[64,512]{1,0:T(8,128)(2,1)} %states_in.1, f32[32,64]{1,0:T(8,128)} %targets_in.1, f32[32,64]{1,0:T(8,128)} %coef_in.1, s32[1,64]{1,0:T(1,128)} %bitcast.1), custom_call_target="tpu_custom_call" | custom-call | tf_op jit(solution)/shard_map/pallas_call | solution.py:447
  62.8 0.6 shard_map.60
